TPU v7x, 256 devices: a whole 4x4x8 slice. The times are simulated.
256 devices in a mesh: grp: 4 (over z_lo), gx: 8 (over y, z_hi), gy: 8 (over x, core).
Axes of the slice: x: 4, y: 4, z: 8 (z_hi: 2, z_lo: 4; z = z_hi * 4 + z_lo), core: 2. Of those that a mesh axis runs over, the one named last changes fastest.
Arguments:
- state: float32 [5, 32, 512, 1024], P(None, 'grp', 'gy', 'gx'), may hold values from -5 to 20, as said below
- tf_table: float32 [4, 4, 256], replicated, may hold values from 0 to 1
- owner: int32 [16, 1], replicated, may hold values from 0 to 3, as said below
- tf_index: int32 [16], replicated, may hold values from 0 to 3
- view_flip: int32 [512], P('gx'), may hold values 0 or 1
Outputs:
- new_state: float32 [5, 32, 512, 1024], P(None, 'grp', 'gy', 'gx')
- slot_image: float32 [32, 4, 512], P('grp', None, ('gx', 'gy'))
Inputs may be any that keep to these rules, and one draw needn't show every extreme that they name: Each render owner is named by at most 8 bricks, and one by exactly 8. `state`: density in component 0 lies between 0.3 and 3, and the implied pressure is positive.
All inputs are finite; a program needn't handle non-finite values. No bound on the sum of `view_flip` on one device may be relied on, other than what follows from the above.
Results may differ from a plain program's by a relative error of at most 0.0003.
Values sent between devices are 32-bit elements; how exact they have to be, the bound alone decides.
No kernel may reach another device: no remote copies, remote signals or barrier semaphores. Data moves between devices by JAX's collectives and lax.ppermute only.
A program may use at most 128 MiB of HBM per device.

v0:
```python
import functools

import jax
import jax.numpy as jnp
import ml_dtypes
import numpy as np
from jax import lax
from jax.experimental import pallas as pl
from jax.experimental.pallas import tpu as pltpu
from jax.sharding import PartitionSpec as P

gamma_less = 0.4
step_size = 0.5
opacity_gain = 6.0
w1, w2, w3, w4 = (0.8, -0.2, 4.0 / 105.0, -1.0 / 280.0)
weights = (w1, w2, w3, w4)

f32 = jnp.float32
VM = pl.BlockSpec(memory_space=pltpu.VMEM)
SM = pl.BlockSpec(memory_space=pltpu.SMEM)


def weight(microseconds):
    return pl.CostEstimate(flops=int(microseconds * 1e9), bytes_accessed=1000000, transcendentals=0)


def params():
    return pltpu.CompilerParams(vmem_limit_bytes=24 * 2**20)


def turn(values, shift, axis):
    size = values.shape[axis]
    shift = shift % size
    return values if shift == 0 else pltpu.roll(values, shift, axis)


def primitives(rho, mx, my, mz, energy):
    inverse = 1.0 / rho
    u, v, w = mx * inverse, my * inverse, mz * inverse
    pressure = gamma_less * (energy - 0.5 * (mx * u + my * v + mz * w))
    return u, v, w, pressure


def east_fields(mx, my, mz, energy, u, v, w, p):
    return mx, mx * u + p, my * u, mz * u, (energy + p) * u, v, w


def north_fields(mx, my, mz, energy, u, v, w, p):
    return my, mx * v, my * v + p, mz * v, (energy + p) * v, u, w


def up_fields(mz, energy, u, v, w, p):
    return mz, mz * u, mz * v, mz * w + p, (energy + p) * w


def first_pack_kernel(state, low, high, y_low, y_high):
    for z in range(8):
        inverse = 1.0 / state[0, z]
        into = low if z < 4 else high
        into[0, z % 4] = state[1, z] * inverse
        into[1, z % 4] = state[2, z] * inverse
    sub = lax.broadcasted_iota(jnp.int32, (8, 128), 0)
    for c in range(5):
        for k in range(4):
            first, second = state[c, 2 * k, 0:8, :], state[c, 2 * k + 1, 0:8, :]
            y_low[c, k] = jnp.where(sub < 4, first, turn(second, 4, 0))
            first, second = state[c, 2 * k, 56:64, :], state[c, 2 * k + 1, 56:64, :]
            y_high[c, k] = jnp.where(sub < 4, turn(first, 4, 0), second)


def second_pack_kernel(state, x_low, x_high):
    lane = lax.broadcasted_iota(jnp.int32, (16, 128), 1)
    slot = lane >> 2
    for c in range(5):
        low = jnp.zeros((16, 128), f32)
        high = jnp.zeros((16, 128), f32)
        for j in range(32):
            row = j % 4 * 16
            moved = turn(state[c, j // 4, row : row + 16, :], 4 * j, 1)
            low = jnp.where(slot == j, moved, low)
            high = jnp.where(slot == (j - 1) % 32, moved, high)
        x_low[c] = low
        x_high[c] = high


def split(f):
    high = f.astype(jnp.bfloat16)
    low = (f - high.astype(f32)).astype(jnp.bfloat16)
    return high, low


def circulant_matrix():
    wide = np.zeros((128, 128), np.float32)
    for lane in range(128):
        for k in range(4):
            wide[(lane + k + 1) % 128, lane] += weights[k]
            wide[(lane - k - 1) % 128, lane] -= weights[k]
    high = wide.astype(ml_dtypes.bfloat16)
    low = (wide - high.astype(np.float32)).astype(ml_dtypes.bfloat16)
    row = np.concatenate([high, low], axis=1)
    return np.concatenate([row, row], axis=0)


def inner_kernel(state, from_south, from_north, matrix, partly, curls, yf, xf, dx):
    for ref, base in ((from_south, 4), (from_north, 72)):
        for k in range(4):
            rho, mx, my, mz, energy = (ref[c, k] for c in range(5))
            fields = north_fields(mx, my, mz, energy, *primitives(rho, mx, my, mz, energy))
            for n in range(7):
                yf[n, 2 * k, base : base + 4, :] = fields[n][0:4]
                yf[n, 2 * k + 1, base : base + 4, :] = fields[n][4:8]

    def plane(z, _):
        for r in range(0, 64, 16):
            rows = slice(r, r + 16)
            rho, mx, my, mz, energy = (state[c, z, rows, :] for c in range(5))
            parts = primitives(rho, mx, my, mz, energy)
            north = north_fields(mx, my, mz, energy, *parts)
            east = east_fields(mx, my, mz, energy, *parts)
            for n in range(7):
                yf[n, z, 8 + r : 24 + r, :] = north[n]
                high, low = split(east[n])
                xf[n, rows, 0:128] = high
                xf[n, rows, 128:256] = low
        for n in range(7):
            both = jnp.dot(xf[n], matrix[...], preferred_element_type=f32)
            dx[n] = both[:, 0:128] + both[:, 128:256]
        for r in range(0, 64, 16):
            rows = slice(r, r + 16)

            def along_y(n):
                total = None
                for k in range(4):
                    upper = yf[n, z, 9 + r + k : 25 + r + k, :]
                    lower = yf[n, z, 7 + r - k : 23 + r - k, :]
                    addend = weights[k] * (upper - lower)
                    total = addend if k == 0 else total + addend
                return total

            for c in range(5):
                partly[c, z, rows, :] = state[c, z, rows, :] - step_size * (dx[c, rows, :] + along_y(c))
            curls[0, z, rows, :] = along_y(6)
            curls[1, z, rows, :] = dx[6, rows, :]
            curls[2, z, rows, :] = dx[5, rows, :] - along_y(5)
        return 0

    lax.fori_loop(0, 8, plane, 0)


def edge_corrections(left_gap, right_gap):
    lane = lax.broadcasted_iota(jnp.int32, (16, 128), 1)
    place = lane & 3
    odd_slot = (lane >> 2 & 1) == 1
    left = jnp.zeros((16, 128), f32)
    right = jnp.zeros((16, 128), f32)
    for i in range(4):
        left += jnp.where(place + i <= 3, weights[3 - i], 0.0) * turn(left_gap, -i, 1)
        right += jnp.where(place >= i, weights[3 - i], 0.0) * turn(right_gap, i, 1)
    right = turn(right, -8, 1)
    return jnp.where(odd_slot, left, right), jnp.where(odd_slot, right, left)


def edge_tile(corrections, chunk):
    lane = lax.broadcasted_iota(jnp.int32, (16, 128), 1)
    fix = turn(corrections[chunk % 2], -4 * (chunk - 1), 1)
    return jnp.where(jnp.logical_or(lane < 4, lane >= 124), fix, 0.0)


def render_kernel(
    ray_total,
    pick,
    flip,
    density_of,
    curls,
    x_low,
    x_high,
    from_left,
    from_right,
    low_a,
    high_a,
    below_a,
    above_a,
    tables,
    segments,
    spins,
):
    def crossing(ref):
        inverse = 1.0 / ref[0]
        return ref[2] * inverse, ref[3] * inverse

    ours_low, ours_high, theirs_low, theirs_high = (
        crossing(r) for r in (x_low, x_high, from_left, from_right)
    )
    v_edge, w_edge = (
        edge_corrections(ours_high[n] - theirs_low[n], theirs_high[n] - ours_low[n]) for n in range(2)
    )
    blocks = (below_a, low_a, high_a, above_a)

    def depth(c, z, rows):
        total = None
        for k in range(4):
            up, down = z + 5 + k, z + 3 - k
            upper = blocks[up // 4][c, up % 4, rows, :]
            lower = blocks[down // 4][c, down % 4, rows, :]
            addend = weights[k] * (upper - lower)
            total = addend if k == 0 else total + addend
        return total

    for z in range(8):
        for b in range(4):
            rows = slice(16 * b, 16 * b + 16)
            chunk = 4 * z + b
            first = curls[0, z, rows, :] - depth(1, z, rows)
            second = depth(0, z, rows) - (curls[1, z, rows, :] + edge_tile(w_edge, chunk))
            third = curls[2, z, rows, :] + edge_tile(v_edge, chunk)
            spins[z, rows, :] = jnp.sqrt(first * first + second * second + third * third)

    flipped = flip[...] == 1
    for i in range(4):
        chosen = pick[i]
        halves = []
        for c in range(4):
            first = jnp.broadcast_to(tables[chosen, c : c + 1, 0:128], (8, 128))
            second = jnp.broadcast_to(tables[chosen, c : c + 1, 128:256], (8, 128))
            last = lax.broadcasted_iota(jnp.int32, (8, 128), 1) == 127
            after_first = jnp.where(last, turn(second, -1, 1), turn(first, -1, 1))
            after_second = jnp.where(last, second, turn(second, -1, 1))
            halves.append((first, second, after_first - first, after_second - second))

        total = None
        for m in range(4):

            def coarse(read):
                gathered = None
                for dz in range(2):
                    for dy in range(2):
                        part = read(2 * i + dz, pl.ds(2 * m + dy, 8, stride=8))
                        gathered = part if gathered is None else gathered + part
                return (gathered + turn(gathered, -1, 1)) * 0.125

            density = coarse(lambda z, rows: density_of[0, z, rows, :])
            spin = coarse(lambda z, rows: spins[z, rows, :])
            coord = 255.0 * jnp.clip((density - 0.9) / 0.6, 0.0, 1.0)
            cell = jnp.minimum(coord.astype(jnp.int32), 255)
            part = coord - cell.astype(f32)
            low_half = cell < 128
            index = cell & 127

            def look(a, b):
                return jnp.where(
                    low_half,
                    jnp.take_along_axis(a, index, axis=1),
                    jnp.take_along_axis(b, index, axis=1),
                )

            entries = [look(h[0], h[1]) + part * look(h[2], h[3]) for h in halves]
            opacity = opacity_gain * entries[3] * spin / (1.0 + spin) / ray_total
            piece = [entries[c] * opacity for c in range(3)] + [1.0 - opacity]
            total = piece if total is None else joined(total, piece, flipped)
        for span in (1, 2, 4):
            later = [turn(t, -span, 0) for t in total]
            total = joined(total, later, flipped)
        lanes = lax.broadcasted_iota(jnp.int32, (8, 128), 1)
        compact = (2 * lanes) & 127
        for c in range(4):
            row = jnp.take_along_axis(total[c], compact, axis=1)
            segments[4 * i + c : 4 * i + c + 1, :] = row[0:1, :]


def joined(near, far, flipped):
    colors = [
        jnp.where(flipped, far[c] + far[3] * near[c], near[c] + near[3] * far[c]) for c in range(3)
    ]
    return colors + [near[3] * far[3]]


def depth_kernel(partly, state, x_low, x_high, from_left, from_right, out, fz):
    def packed(ref):
        rho, mx, my, mz, energy = (ref[c] for c in range(5))
        return east_fields(mx, my, mz, energy, *primitives(rho, mx, my, mz, energy))[:5]

    ours_low, ours_high = packed(x_low), packed(x_high)
    theirs_low, theirs_high = packed(from_left), packed(from_right)
    edges = [
        edge_corrections(ours_high[n] - theirs_low[n], theirs_high[n] - ours_low[n]) for n in range(5)
    ]
    for z in range(8):
        for r in range(0, 64, 16):
            rows = slice(r, r + 16)
            rho, mx, my, mz, energy = (state[c, z, rows, :] for c in range(5))
            fields = up_fields(mz, energy, *primitives(rho, mx, my, mz, energy))
            for c in range(5):
                fz[c, z, rows, :] = fields[c]
    for c in range(5):
        for z in range(8):
            for b in range(4):
                rows = slice(16 * b, 16 * b + 16)
                total = edge_tile(edges[c], 4 * z + b)
                for k in range(4):
                    if z + k + 1 < 8:
                        total = total + weights[k] * fz[c, z + k + 1, rows, :]
                    if z - k - 1 >= 0:
                        total = total - weights[k] * fz[c, z - k - 1, rows, :]
                out[c, z, rows, :] = partly[c, z, rows, :] - step_size * total


def last_kernel(partly, below_a, below_b, above_a, above_b, out, fz):
    for side, (a, b) in enumerate(((below_a, below_b), (above_a, above_b))):
        for p in range(4):
            for r in range(0, 64, 16):
                rows = slice(r, r + 16)
                u, v = a[0, p, rows, :], a[1, p, rows, :]
                rho, mz, energy = b[0, p, rows, :], b[1, p, rows, :], b[2, p, rows, :]
                w = mz / rho
                pressure = gamma_less * (energy - 0.5 * (rho * (u * u + v * v) + mz * w))
                fields = up_fields(mz, energy, u, v, w, pressure)
                for c in range(5):
                    fz[c, 4 * side + p, rows, :] = step_size * fields[c]
    for c in range(5):
        for z in range(8):
            for r in range(0, 64, 16):
                rows = slice(r, r + 16)
                total = partly[c, z, rows, :]
                for k in range(4):
                    if z + k + 1 >= 8:
                        total = total - weights[k] * fz[c, 4 + z + k + 1 - 8, rows, :]
                    if z - k - 1 < 0:
                        total = total + weights[k] * fz[c, z - k - 1 + 4, rows, :]
                out[c, z, rows, :] = total


def compose_kernel(me, owner, flip, pieces, out):
    lane = lax.broadcasted_iota(jnp.int32, (4, 128), 1)
    channel = lane >> 3 & 3
    flipped = flip[...] == 1

    def passing(x):
        return jnp.where(
            channel == 3,
            x,
            jnp.where(
                channel == 2, turn(x, -8, 1), jnp.where(channel == 1, turn(x, -16, 1), turn(x, -24, 1))
            ),
        )

    total = pieces[:, 0, :]
    total_pass = passing(total)
    for j in range(1, 8):
        later = pieces[:, j, :]
        later_pass = passing(later)
        both = total_pass * later_pass
        color = jnp.where(flipped, later + later_pass * total, total + total_pass * later)
        total = jnp.where(channel == 3, both, color)
        total_pass = both
    total = jnp.where(channel == 3, 1.0 - total, total)
    sub = lax.broadcasted_iota(jnp.int32, (8, 128), 0)
    result = jnp.zeros((8, 128), f32)
    count = jnp.int32(0)
    shifted = [turn(total, -32 * i, 1) for i in range(4)]
    for b in range(16):
        mine = owner[b] == me[0]
        slot = jnp.where(mine, count, -1)
        count = jnp.where(mine, count + 1, count)
        row = jnp.broadcast_to(shifted[b % 4][b // 4 : b // 4 + 1, :], (8, 128))
        result = jnp.where(sub == slot, row, result)
    for c in range(4):
        out[:, c, :] = turn(result, -8 * c, 1)[:, 0:8]


def shape(*dims):
    return jax.ShapeDtypeStruct(dims, f32)


def ring(axis, step):
    count = lax.axis_size(axis)
    return [(i, (i + step) % count) for i in range(count)]


def after(value, *others):
    return lax.optimization_barrier((value, *others))[0]


def local(state, tf_table, owner, tf_index, view_flip):
    grp = lax.axis_index("grp")
    gy = lax.axis_index("gy")
    groups, depth = lax.axis_size("grp"), lax.axis_size("gy")
    low_a, high_a, y_low, y_high = pl.pallas_call(
        first_pack_kernel,
        out_shape=(shape(2, 4, 64, 128), shape(2, 4, 64, 128), shape(5, 4, 8, 128), shape(5, 4, 8, 128)),
        in_specs=[VM],
        out_specs=(VM, VM, VM, VM),
        compiler_params=params(),
    )(state)
    from_below_a = lax.ppermute(high_a, "grp", ring("grp", 1))
    from_above_a = lax.ppermute(low_a, "grp", ring("grp", -1))
    from_south = lax.ppermute(y_high, "gy", ring("gy", 1))
    from_north = lax.ppermute(y_low, "gy", ring("gy", -1))
    x_low, x_high = pl.pallas_call(
        second_pack_kernel,
        out_shape=(shape(5, 16, 128), shape(5, 16, 128)),
        in_specs=[VM],
        out_specs=(VM, VM),
        compiler_params=params(),
    )(after(state, y_low))
    from_left = lax.ppermute(x_high, "gx", ring("gx", 1))
    from_right = lax.ppermute(x_low, "gx", ring("gx", -1))
    partly, curls = pl.pallas_call(
        inner_kernel,
        out_shape=(shape(5, 8, 64, 128), shape(3, 8, 64, 128)),
        in_specs=[VM] * 4,
        out_specs=(VM, VM),
        scratch_shapes=[
            pltpu.VMEM((7, 8, 80, 128), f32),
            pltpu.VMEM((7, 64, 256), jnp.bfloat16),
            pltpu.VMEM((7, 64, 128), f32),
        ],
        compiler_params=params(),
        cost_estimate=weight(1),
    )(state, from_south, from_north, jnp.asarray(circulant_matrix()))

    late = after(state, from_above_a, from_below_a)
    from_above_b = lax.ppermute(jnp.stack([late[c, :4] for c in (0, 3, 4)]), "grp", ring("grp", -1))
    from_below_b = lax.ppermute(jnp.stack([late[c, 4:] for c in (0, 3, 4)]), "grp", ring("grp", 1))

    pick = lax.dynamic_slice_in_dim(tf_index, grp * 4, 4)
    flip = jnp.repeat(view_flip, 2)[None, :]
    segments = pl.pallas_call(
        functools.partial(render_kernel, float(depth * 32)),
        out_shape=shape(16, 128),
        in_specs=[SM] + [VM] * 12,
        out_specs=VM,
        scratch_shapes=[pltpu.VMEM((8, 64, 128), f32)],
        compiler_params=params(),
        cost_estimate=weight(60),
    )(
        pick, flip, state, curls, x_low, x_high, from_left, from_right,
        low_a, high_a, from_below_a, from_above_a, tf_table,
    )
    width = 64 // depth
    pieces = segments[:, :64].reshape(16, depth, width).transpose(1, 0, 2).reshape(depth, 16 * width)
    sent = jnp.tile(pieces, (groups, 1))
    received = lax.all_to_all(sent, ("grp", "gy"), 0, 0, tiled=True).reshape(groups, depth, 128)
    most = pl.pallas_call(
        depth_kernel,
        out_shape=shape(5, 8, 64, 128),
        in_specs=[VM] * 6,
        out_specs=VM,
        scratch_shapes=[pltpu.VMEM((5, 8, 64, 128), f32)],
        compiler_params=params(),
    )(after(partly, segments), state, x_low, x_high, from_left, from_right)
    new_state = pl.pallas_call(
        last_kernel,
        out_shape=shape(5, 8, 64, 128),
        in_specs=[VM] * 5,
        out_specs=VM,
        scratch_shapes=[pltpu.VMEM((5, 8, 64, 128), f32)],
        compiler_params=params(),
    )(most, from_below_a, from_below_b, from_above_a, from_above_b)
    own_flip = jnp.tile(lax.dynamic_slice_in_dim(view_flip, gy * width, width), 16)[None, :]
    image = pl.pallas_call(
        compose_kernel,
        out_shape=shape(8, 4, 8),
        in_specs=[SM, SM, VM, VM],
        out_specs=VM,
        compiler_params=params(),
    )(grp[None], owner[:, 0], own_flip, received)
    return (new_state, image)


def solution(mesh):
    placed = (P(None, "grp", "gy", "gx"), P(), P(), P(), P("gx"))
    return jax.shard_map(
        local,
        mesh=mesh,
        in_specs=placed,
        out_specs=(P(None, "grp", "gy", "gx"), P("grp", None, ("gx", "gy"))),
        check_vma=False,
    )
```

profile of v0, /device:TPU:1, one launch (start us, length us, event | category | flops | bytes accessed | tf_op | source)
XLA Modules:
  0.0 51.9 jit_solution(5724956123547801906)
XLA Ops:
  0.6 1.3 %copy-done = f32[5,8,64,128]{3,2,1,0:T(8,128)S(1)} copy-done((f32[5,8,64,128]{3,2,1,0:T(8,128)S(1)}, f32[5,8,64,128]{3,2,1,0:T(8,128)}, u32[]{:S(2)}) %copy-start) | copy-done | bytes 1310744
  2.0 2.5 %collective-permute-start.4 = (f32[2,4,64,128]{3,2,1,0:T(8,128)S(1)}, f32[2,4,64,128]{3,2,1,0:T(8,128)S(1)}, u32[]{:S(2)}, u32[]{:S(2)}) collective-permute-start(f32[2,4,64,128]{3,2,1,0:T(8,128)S(1)} %get-tuple-element.21.high_a), channel_id=1, source_target_pairs={{0,64},{64,128},{128,192},{192,0},{1,65},{65,129},{129,193},{193,1... | collective-permute-start | bytes 786440 | tf_op jit(solution)/shard_map/ppermute | solution.py:394
  4.6 2.8 %collective-permute-start.5 = (f32[2,4,64,128]{3,2,1,0:T(8,128)S(1)}, f32[2,4,64,128]{3,2,1,0:T(8,128)S(1)}, u32[]{:S(2)}, u32[]{:S(2)}) collective-permute-start(f32[2,4,64,128]{3,2,1,0:T(8,128)S(1)} %get-tuple-element.20.low_a), channel_id=1, source_target_pairs={{0,192},{64,0},{128,64},{192,128},{1,193},{65,1},{129,65},{193,129... | collective-permute-start | bytes 786440 | tf_op jit(solution)/shard_map/ppermute | solution.py:395
  7.4 1.8 %collective-permute-start.1 = (f32[5,4,8,128]{3,2,1,0:T(8,128)S(1)}, f32[5,4,8,128]{3,2,1,0:T(8,128)S(1)}, u32[]{:S(2)}, u32[]{:S(2)}) collective-permute-start(f32[5,4,8,128]{3,2,1,0:T(8,128)S(1)} %get-tuple-element.14), channel_id=1, source_target_pairs={{0,7},{1,0},{2,1},{3,2},{4,3},{5,4},{6,5},{7,6},{8,15},{9,8},{10,9... | collective-permute-start | bytes 245768 | tf_op jit(solution)/shard_map/ppermute | solution.py:397
  9.2 0.3 collective-permute-start
  9.4 0.4 shard_map.79
  9.8 6.1 %collective-permute-start.2 = (f32[5,16,128]{2,1,0:T(8,128)S(1)}, f32[5,16,128]{2,1,0:T(8,128)S(1)}, u32[]{:S(2)}, u32[]{:S(2)}) collective-permute-start(f32[5,16,128]{2,1,0:T(8,128)S(1)} %get-tuple-element.19.x_high), channel_id=1, source_target_pairs={{0,8},{8,16},{16,24},{24,32},{32,40},{40,48},{48,56},{56,0},{1,9},... | collective-permute-start | bytes 122888 | tf_op jit(solution)/shard_map/ppermute | solution.py:405
  16.0 0.1 broadcast_in_dim_reshape.3.flip
  16.2 4.1 %collective-permute-start.3 = (f32[5,16,128]{2,1,0:T(8,128)S(1)}, f32[5,16,128]{2,1,0:T(8,128)S(1)}, u32[]{:S(2)}, u32[]{:S(2)}) collective-permute-start(f32[5,16,128]{2,1,0:T(8,128)S(1)} %get-tuple-element.18.x_low), channel_id=1, source_target_pairs={{0,56},{8,0},{16,8},{24,16},{32,24},{40,32},{48,40},{56,48},{1,57}... | collective-permute-start | bytes 122888 | tf_op jit(solution)/shard_map/ppermute | solution.py:406
  20.3 2.4 %shard_map.78 = (f32[5,8,64,128]{3,2,1,0:T(8,128)S(1)}, f32[3,8,64,128]{3,2,1,0:T(8,128)S(1)}) custom-call(f32[5,8,64,128]{3,2,1,0:T(8,128)S(1)} %copy-done.1, f32[5,4,8,128]{3,2,1,0:T(8,128)S(1)} %collective-permute-done.from_south, f32[5,4,8,128]{3,2,1,0:T(8,128)S(1)} %collective-permute-done.1.from_north, bf16[256,256]{1,0:T(8,128)(2,1)S(1)} %copy-done.12), custom_call_target="tpu_custom_call" | custom-call | flops 1000000000 | bytes 1000000 | tf_op jit(solution)/shard_map/pallas_call | solution.py:407
  22.9 1.0 %pad_maximum_fusion = f32[3,4,64,128]{3,2,1,0:T(8,128)} fusion(f32[2,4,64,128]{3,2,1,0:T(8,128)S(1)} %get-tuple-element.27, f32[1,4,64,128]{3,2,1,0:T(8,128)S(1)} %get-tuple-element.25), kind=kLoop, calls=%fused_computation | loop fusion | flops 98304 | bytes 786432 | tf_op jit(solution)/shard_map/stack | solution.py:423
  23.8 0.8 %pad_maximum_fusion.1 = f32[3,4,64,128]{3,2,1,0:T(8,128)} fusion(f32[2,4,64,128]{3,2,1,0:T(8,128)S(1)} %get-tuple-element.26, f32[1,4,64,128]{3,2,1,0:T(8,128)S(1)} %get-tuple-element.24), kind=kLoop, calls=%fused_computation.1 | loop fusion | flops 98304 | bytes 786432 | tf_op jit(solution)/shard_map/stack | solution.py:422
  24.6 3.3 %collective-permute-start.7 = (f32[3,4,64,128]{3,2,1,0:T(8,128)}, f32[3,4,64,128]{3,2,1,0:T(8,128)S(1)}, u32[]{:S(2)}, u32[]{:S(2)}) collective-permute-start(f32[3,4,64,128]{3,2,1,0:T(8,128)} %pad_maximum_fusion.1), channel_id=1, source_target_pairs={{0,192},{64,0},{128,64},{192,128},{1,193},{65,1},{129,65},{193,129... | collective-permute-start | bytes 1179656 | tf_op jit(solution)/shard_map/ppermute | solution.py:422
  27.9 2.7 %shard_map.80 = f32[16,128]{1,0:T(8,128)S(1)} custom-call(s32[4]{0:T(128)S(1)} %dynamic_slice.6.pick, s32[1,128]{1,0:T(1,128)S(1)} %broadcast_in_dim_reshape.3.flip, f32[5,8,64,128]{3,2,1,0:T(8,128)S(1)} %copy-done.1, f32[3,8,64,128]{3,2,1,0:T(8,128)S(1)} %get-tuple-element.16.curls, f32[5,16,128]{2,1,0:T(8,128)S(1)} %get-tuple-element.18.x_low, ...), custom_call_target="tpu_custom_call" | custom-call | flops 60000002048 | bytes 1000000 | tf_op jit(solution)/shard_map/pallas_call | solution.py:427
  30.9 0.6 %tile.16 = f32[4,8,128]{2,1,0:T(8,128)} broadcast(f32[8,128]{1,0:T(8,128)S(1)} %tile.7), dimensions={1,2} | broadcast | bytes 20480 | tf_op jit(solution)/shard_map/tile | solution.py:441
  31.5 7.8 %all-to-all-start = ((f32[32,1,128]{2,1,0:T(1,128)}), f32[32,1,128]{2,1,0:T(1,128)S(1)}, u32[]{:S(2)}, u32[]{:S(2)}) async-start(f32[32,1,128]{2,1,0:T(1,128)} %bitcast.4), calls=%async_computation | async-start | bytes 32768 | tf_op jit(solution)/shard_map/all_to_all | solution.py:442
  39.6 1.3 %copy-done.3 = f32[5,8,64,128]{3,2,1,0:T(8,128)S(1)} copy-done((f32[5,8,64,128]{3,2,1,0:T(8,128)S(1)}, f32[5,8,64,128]{3,2,1,0:T(8,128)}, u32[]{:S(2)}) %copy-start.3) | copy-done | bytes 1310744
  40.9 0.8 %copy-done.9 = f32[5,16,128]{2,1,0:T(8,128)S(1)} copy-done((f32[5,16,128]{2,1,0:T(8,128)S(1)}, f32[5,16,128]{2,1,0:T(8,128)}, u32[]{:S(2)}) %copy-start.9) | copy-done | bytes 40984
  41.7 1.0 %shard_map.81.partly = f32[5,8,64,128]{3,2,1,0:T(8,128)S(1)} custom-call(f32[5,8,64,128]{3,2,1,0:T(8,128)S(1)} %copy-done.3, f32[5,8,64,128]{3,2,1,0:T(8,128)S(1)} %copy-done.1, f32[5,16,128]{2,1,0:T(8,128)S(1)} %get-tuple-element.18.x_low, f32[5,16,128]{2,1,0:T(8,128)S(1)} %get-tuple-element.19.x_high, f32[5,16,128]{2,1,0:T(8,128)S(1)} %collective-permute-done.2.from_left, ...), custom_call_target="tpu_custom_call" | custom-call | tf_op jit(solution)/shard_map/pallas_call | solution.py:443
  42.7 4.4 %all-to-all-done = f32[32,1,128]{2,1,0:T(1,128)S(1)} async-done(((f32[32,1,128]{2,1,0:T(1,128)}), f32[32,1,128]{2,1,0:T(1,128)S(1)}, u32[]{:S(2)}, u32[]{:S(2)}) %all-to-all-start) | async-done | bytes 16416 | tf_op jit(solution)/shard_map/all_to_all | solution.py:442
  47.0 1.4 %shard_map.83 = f32[8,4,8]{2,1,0:T(4,128)} custom-call(s32[1]{0:T(128)} %bitcast.me, s32[16]{0:T(128)S(1)} %bitcast.10, s32[1,128]{1,0:T(1,128)S(1)} %broadcast_in_dim_tile.3.flip, f32[4,8,128]{2,1,0:T(8,128)S(1)} %bitcast.8), custom_call_target="tpu_custom_call" | custom-call | tf_op jit(solution)/shard_map/pallas_call | solution.py:460
  48.5 0.9 %copy-done.5 = f32[2,4,64,128]{3,2,1,0:T(8,128)S(1)} copy-done((f32[2,4,64,128]{3,2,1,0:T(8,128)S(1)}, f32[2,4,64,128]{3,2,1,0:T(8,128)}, u32[]{:S(2)}) %copy-start.5) | copy-done | bytes 262168
  49.4 0.9 %copy-done.7 = f32[2,4,64,128]{3,2,1,0:T(8,128)S(1)} copy-done((f32[2,4,64,128]{3,2,1,0:T(8,128)S(1)}, f32[2,4,64,128]{3,2,1,0:T(8,128)}, u32[]{:S(2)}) %copy-start.7) | copy-done | bytes 262168
  50.4 1.5 %shard_map.82 = f32[5,8,64,128]{3,2,1,0:T(8,128)} custom-call(f32[5,8,64,128]{3,2,1,0:T(8,128)S(1)} %shard_map.81.partly, f32[2,4,64,128]{3,2,1,0:T(8,128)S(1)} %copy-done.5, f32[3,4,64,128]{3,2,1,0:T(8,128)S(1)} %collective-permute-done.6.below_b, f32[2,4,64,128]{3,2,1,0:T(8,128)S(1)} %copy-done.7, f32[3,4,64,128]{3,2,1,0:T(8,128)S(1)} %collective-permute-done.7.above_b), custom_call_target="tpu_custom_call" | custom-call | tf_op jit(solution)/shard_map/pallas_call | solution.py:451
  (45 shorter events, 0.8 us)
Async XLA Ops:
  0.6 1.3 %copy-start = (f32[5,8,64,128]{3,2,1,0:T(8,128)S(1)}, f32[5,8,64,128]{3,2,1,0:T(8,128)}, u32[]{:S(2)}) copy-start(f32[5,8,64,128]{3,2,1,0:T(8,128)} %state.6) | copy-start | bytes 3932164
  1.9 14.0 %copy-start.13 = (s32[64]{0:T(128)S(1)}, s32[64]{0:T(128)}, u32[]{:S(2)}) copy-start(s32[64]{0:T(128)} %param.10) | copy-start | bytes 772
  1.9 14.2 %copy-start.14 = (s32[16]{0:T(128)S(1)}, s32[16]{0:T(128)}, u32[]{:S(2)}) copy-start(s32[16]{0:T(128)} %param.9) | copy-start | bytes 196
  2.0 18.4 %copy-start.1 = (f32[5,8,64,128]{3,2,1,0:T(8,128)S(1)}, f32[5,8,64,128]{3,2,1,0:T(8,128)}, u32[]{:S(2)}) copy-start(f32[5,8,64,128]{3,2,1,0:T(8,128)} %state.6) | copy-start | bytes 3932164
  2.0 18.4 %copy-start.12 = (bf16[256,256]{1,0:T(8,128)(2,1)S(1)}, bf16[256,256]{1,0:T(8,128)(2,1)}, u32[]{:S(2)}) copy-start(bf16[256,256]{1,0:T(8,128)(2,1)} %constant.22.clone.matrix) | copy-start | bytes 393220
  2.0 20.7 %collective-permute-start.4 = (f32[2,4,64,128]{3,2,1,0:T(8,128)S(1)}, f32[2,4,64,128]{3,2,1,0:T(8,128)S(1)}, u32[]{:S(2)}, u32[]{:S(2)}) collective-permute-start(f32[2,4,64,128]{3,2,1,0:T(8,128)S(1)} %get-tuple-element.21.high_a), channel_id=1, source_target_pairs={{0,64},{64,128},{128,192},{192,0},{1,65},{65,129},{129,193},{193,1... | collective-permute-start | bytes 786440 | tf_op jit(solution)/shard_map/ppermute | solution.py:394
  4.6 18.2 %collective-permute-start.5 = (f32[2,4,64,128]{3,2,1,0:T(8,128)S(1)}, f32[2,4,64,128]{3,2,1,0:T(8,128)S(1)}, u32[]{:S(2)}, u32[]{:S(2)}) collective-permute-start(f32[2,4,64,128]{3,2,1,0:T(8,128)S(1)} %get-tuple-element.20.low_a), channel_id=1, source_target_pairs={{0,192},{64,0},{128,64},{192,128},{1,193},{65,1},{129,65},{193,129... | collective-permute-start | bytes 786440 | tf_op jit(solution)/shard_map/ppermute | solution.py:395
  7.4 8.9 %collective-permute-start.1 = (f32[5,4,8,128]{3,2,1,0:T(8,128)S(1)}, f32[5,4,8,128]{3,2,1,0:T(8,128)S(1)}, u32[]{:S(2)}, u32[]{:S(2)}) collective-permute-start(f32[5,4,8,128]{3,2,1,0:T(8,128)S(1)} %get-tuple-element.14), channel_id=1, source_target_pairs={{0,7},{1,0},{2,1},{3,2},{4,3},{5,4},{6,5},{7,6},{8,15},{9,8},{10,9... | collective-permute-start | bytes 245768 | tf_op jit(solution)/shard_map/ppermute | solution.py:397
  9.2 11.1 %collective-permute-start = (f32[5,4,8,128]{3,2,1,0:T(8,128)S(1)}, f32[5,4,8,128]{3,2,1,0:T(8,128)S(1)}, u32[]{:S(2)}, u32[]{:S(2)}) collective-permute-start(f32[5,4,8,128]{3,2,1,0:T(8,128)S(1)} %get-tuple-element.13), channel_id=1, source_target_pairs={{0,1},{1,2},{2,3},{3,4},{4,5},{5,6},{6,7},{7,0},{8,9},{9,10},{10,1... | collective-permute-start | bytes 245768 | tf_op jit(solution)/shard_map/ppermute | solution.py:396
  9.8 18.0 %collective-permute-start.2 = (f32[5,16,128]{2,1,0:T(8,128)S(1)}, f32[5,16,128]{2,1,0:T(8,128)S(1)}, u32[]{:S(2)}, u32[]{:S(2)}) collective-permute-start(f32[5,16,128]{2,1,0:T(8,128)S(1)} %get-tuple-element.19.x_high), channel_id=1, source_target_pairs={{0,8},{8,16},{16,24},{24,32},{32,40},{40,48},{48,56},{56,0},{1,9},... | collective-permute-start | bytes 122888 | tf_op jit(solution)/shard_map/ppermute | solution.py:405
  16.2 11.6 %collective-permute-start.3 = (f32[5,16,128]{2,1,0:T(8,128)S(1)}, f32[5,16,128]{2,1,0:T(8,128)S(1)}, u32[]{:S(2)}, u32[]{:S(2)}) collective-permute-start(f32[5,16,128]{2,1,0:T(8,128)S(1)} %get-tuple-element.18.x_low), channel_id=1, source_target_pairs={{0,56},{8,0},{16,8},{24,16},{32,24},{40,32},{48,40},{56,48},{1,57}... | collective-permute-start | bytes 122888 | tf_op jit(solution)/shard_map/ppermute | solution.py:406
  22.7 1.9 %copy-start.2 = (f32[5,8,64,128]{3,2,1,0:T(8,128)}, f32[5,8,64,128]{3,2,1,0:T(8,128)S(1)}, u32[]{:S(2)}) copy-start(f32[5,8,64,128]{3,2,1,0:T(8,128)S(1)} %get-tuple-element.22.partly) | copy-start | bytes 3932164
  22.7 5.1 %copy-start.4 = (f32[2,4,64,128]{3,2,1,0:T(8,128)}, f32[2,4,64,128]{3,2,1,0:T(8,128)S(1)}, u32[]{:S(2)}) copy-start(f32[2,4,64,128]{3,2,1,0:T(8,128)S(1)} %collective-permute-done.4.below_a) | copy-start | bytes 786436
  22.8 5.1 %copy-start.6 = (f32[2,4,64,128]{3,2,1,0:T(8,128)}, f32[2,4,64,128]{3,2,1,0:T(8,128)S(1)}, u32[]{:S(2)}) copy-start(f32[2,4,64,128]{3,2,1,0:T(8,128)S(1)} %collective-permute-done.5.above_a) | copy-start | bytes 786436
  22.8 5.1 %copy-start.11 = (f32[4,4,256]{2,1,0:T(4,128)S(1)}, f32[4,4,256]{2,1,0:T(4,128)}, u32[]{:S(2)}) copy-start(f32[4,4,256]{2,1,0:T(4,128)} %tables.1) | copy-start | bytes 49156
  23.8 24.6 %collective-permute-start.6 = (f32[3,4,64,128]{3,2,1,0:T(8,128)}, f32[3,4,64,128]{3,2,1,0:T(8,128)S(1)}, u32[]{:S(2)}, u32[]{:S(2)}) collective-permute-start(f32[3,4,64,128]{3,2,1,0:T(8,128)} %pad_maximum_fusion), channel_id=1, source_target_pairs={{0,64},{64,128},{128,192},{192,0},{1,65},{65,129},{129,193},{193,1... | collective-permute-start | bytes 1179656 | tf_op jit(solution)/shard_map/ppermute | solution.py:423
  24.6 23.8 %collective-permute-start.7 = (f32[3,4,64,128]{3,2,1,0:T(8,128)}, f32[3,4,64,128]{3,2,1,0:T(8,128)S(1)}, u32[]{:S(2)}, u32[]{:S(2)}) collective-permute-start(f32[3,4,64,128]{3,2,1,0:T(8,128)} %pad_maximum_fusion.1), channel_id=1, source_target_pairs={{0,192},{64,0},{128,64},{192,128},{1,193},{65,1},{129,65},{193,129... | collective-permute-start | bytes 1179656 | tf_op jit(solution)/shard_map/ppermute | solution.py:422
  27.9 2.8 %copy-start.8 = (f32[5,16,128]{2,1,0:T(8,128)}, f32[5,16,128]{2,1,0:T(8,128)S(1)}, u32[]{:S(2)}) copy-start(f32[5,16,128]{2,1,0:T(8,128)S(1)} %collective-permute-done.3.from_right) | copy-start | bytes 122884
  31.5 15.5 %all-to-all-start = ((f32[32,1,128]{2,1,0:T(1,128)}), f32[32,1,128]{2,1,0:T(1,128)S(1)}, u32[]{:S(2)}, u32[]{:S(2)}) async-start(f32[32,1,128]{2,1,0:T(1,128)} %bitcast.4), calls=%async_computation | async-start | bytes 32768 | tf_op jit(solution)/shard_map/all_to_all | solution.py:442
  39.6 1.3 %copy-start.3 = (f32[5,8,64,128]{3,2,1,0:T(8,128)S(1)}, f32[5,8,64,128]{3,2,1,0:T(8,128)}, u32[]{:S(2)}) copy-start(f32[5,8,64,128]{3,2,1,0:T(8,128)} %copy-done.2) | copy-start | bytes 3932164
  40.9 0.8 %copy-start.9 = (f32[5,16,128]{2,1,0:T(8,128)S(1)}, f32[5,16,128]{2,1,0:T(8,128)}, u32[]{:S(2)}) copy-start(f32[5,16,128]{2,1,0:T(8,128)} %copy-done.8) | copy-start | bytes 122884
  41.7 5.4 %copy-start.10 = (s32[16,1]{0,1:T(1,128)S(1)}, s32[16,1]{0,1:T(1,128)}, u32[]{:S(2)}) copy-start(s32[16,1]{0,1:T(1,128)} %param.8) | copy-start | bytes 196
  48.4 1.0 %copy-start.5 = (f32[2,4,64,128]{3,2,1,0:T(8,128)S(1)}, f32[2,4,64,128]{3,2,1,0:T(8,128)}, u32[]{:S(2)}) copy-start(f32[2,4,64,128]{3,2,1,0:T(8,128)} %copy-done.4) | copy-start | bytes 786436
  49.4 0.9 %copy-start.7 = (f32[2,4,64,128]{3,2,1,0:T(8,128)S(1)}, f32[2,4,64,128]{3,2,1,0:T(8,128)}, u32[]{:S(2)}) copy-start(f32[2,4,64,128]{3,2,1,0:T(8,128)} %copy-done.6) | copy-start | bytes 786436
where the time goes:
time: 52.2 us; the launch traced here: 51.9 us
  starting transfers between devices  28.7 us (55%)
  Pallas kernels  9.51 us (18%)
  local copies, waits for them, and re-layouts  6.73 us (13%)
  waiting for transfers between devices  4.4 us (8%)
  other arithmetic  1.74 us (3%)
  between operations  0.82 us (2%)
    all_to_all x1, starting transfers between devices, local(): lax.all_to_all(sent, ('grp', 'gy'), 0, 0, tiled=True)  7.84 us
    ppermute x1, starting transfers between devices, local(): from_left = lax.ppermute(x_high, 'gx', ring('gx', 1))  6.1 us
    unnamed x30, local copies, waits for them, and re-layouts  5.34 us
    all_to_all x1, waiting for transfers between devices, local(): lax.all_to_all(sent, ('grp', 'gy'), 0, 0, tiled=True)  4.38 us
    ppermute x1, starting transfers between devices, local(): from_right = lax.ppermute(x_low, 'gx', ring('gx', -1))  4.06 us
    ppermute x1, starting transfers between devices, local(): lax.ppermute(jnp.stack([late[c, :4] for c in (0, 3, 4)]), 'grp', ring('gr...  3.26 us
    ppermute x1, starting transfers between devices, local(): from_above_a = lax.ppermute(low_a, 'grp', ring('grp', -1))  2.8 us
    pallas_call x1, Pallas kernels, local(): pl.pallas_call(functools.partial(render_kernel, float(depth * 32)), out_s...  2.74 us
  transfers between devices with their start and end apart: 9, of which 1 were waited for; matrix products, arithmetic and copies ran while one was open for 6% of the time, Pallas kernels for 15%

commit v1 on v0

--- a/solution.py
+++ b/solution.py
@@ -2,8 +2,6 @@
 
 import jax
 import jax.numpy as jnp
-import ml_dtypes
-import numpy as np
 from jax import lax
 from jax.experimental import pallas as pl
 from jax.experimental.pallas import tpu as pltpu
@@ -18,14 +16,19 @@
 f32 = jnp.float32
 VM = pl.BlockSpec(memory_space=pltpu.VMEM)
 SM = pl.BlockSpec(memory_space=pltpu.SMEM)
+HB = pl.BlockSpec(memory_space=pltpu.HBM)
 
 
 def weight(microseconds):
     return pl.CostEstimate(flops=int(microseconds * 1e9), bytes_accessed=1000000, transcendentals=0)
 
 
-def params():
-    return pltpu.CompilerParams(vmem_limit_bytes=24 * 2**20)
+def params(mebibytes=2):
+    return pltpu.CompilerParams(vmem_limit_bytes=mebibytes * 2**20)
+
+
+def in_hbm(a):
+    return pltpu.with_memory_space_constraint(a, pltpu.HBM)
 
 
 def turn(values, shift, axis):
@@ -83,25 +86,55 @@
         x_high[c] = high
 
 
+def third_pack_kernel(state, low_b, high_b):
+    for n, c in enumerate((0, 3, 4)):
+        low_b[n] = state[c, :4]
+        high_b[n] = state[c, 4:]
+
+
 def split(f):
     high = f.astype(jnp.bfloat16)
     low = (f - high.astype(f32)).astype(jnp.bfloat16)
     return high, low
 
 
-def circulant_matrix():
-    wide = np.zeros((128, 128), np.float32)
-    for lane in range(128):
-        for k in range(4):
-            wide[(lane + k + 1) % 128, lane] += weights[k]
-            wide[(lane - k - 1) % 128, lane] -= weights[k]
-    high = wide.astype(ml_dtypes.bfloat16)
-    low = (wide - high.astype(np.float32)).astype(ml_dtypes.bfloat16)
-    row = np.concatenate([high, low], axis=1)
-    return np.concatenate([row, row], axis=0)
-
-
-def inner_kernel(state, from_south, from_north, matrix, partly, curls, yf, xf, dx):
+def write_circulant(matrix):
+    row = lax.broadcasted_iota(jnp.int32, (128, 128), 0)
+    column = lax.broadcasted_iota(jnp.int32, (128, 128), 1)
+    offset = (row - column) & 127
+    wide = jnp.zeros((128, 128), f32)
+    for k in range(4):
+        wide = jnp.where(offset == k + 1, weights[k], wide)
+        wide = jnp.where(offset == 127 - k, -weights[k], wide)
+    high, low = split(wide)
+    for half in (slice(0, 128), slice(128, 256)):
+        matrix[half, 0:128] = high
+        matrix[half, 128:256] = low
+
+
+def inner_kernel(
+    state, from_south, from_north, partly, curls, matrix, yf, xf, dx
+):
+    write_circulant(matrix)
+
+    def fields_of(z, _):
+        for r in range(0, 64, 16):
+            rows = slice(r, r + 16)
+            rho, mx, my, mz, energy = (state[c, z, rows, :] for c in range(5))
+            parts = primitives(rho, mx, my, mz, energy)
+            north_parts = north_fields(mx, my, mz, energy, *parts)
+            east_parts = east_fields(mx, my, mz, energy, *parts)
+            for n in range(7):
+                yf[n, z, 8 + r : 24 + r, :] = north_parts[n]
+                high, low = split(east_parts[n])
+                xf[n, rows, 0:128] = high
+                xf[n, rows, 128:256] = low
+        for n in range(7):
+            both = jnp.dot(xf[n], matrix[...], preferred_element_type=f32)
+            dx[n, z] = both[:, 0:128] + both[:, 128:256]
+        return 0
+
+    lax.fori_loop(0, 8, fields_of, 0)
     for ref, base in ((from_south, 4), (from_north, 72)):
         for k in range(4):
             rho, mx, my, mz, energy = (ref[c, k] for c in range(5))
@@ -111,20 +144,6 @@
                 yf[n, 2 * k + 1, base : base + 4, :] = fields[n][4:8]
 
     def plane(z, _):
-        for r in range(0, 64, 16):
-            rows = slice(r, r + 16)
-            rho, mx, my, mz, energy = (state[c, z, rows, :] for c in range(5))
-            parts = primitives(rho, mx, my, mz, energy)
-            north = north_fields(mx, my, mz, energy, *parts)
-            east = east_fields(mx, my, mz, energy, *parts)
-            for n in range(7):
-                yf[n, z, 8 + r : 24 + r, :] = north[n]
-                high, low = split(east[n])
-                xf[n, rows, 0:128] = high
-                xf[n, rows, 128:256] = low
-        for n in range(7):
-            both = jnp.dot(xf[n], matrix[...], preferred_element_type=f32)
-            dx[n] = both[:, 0:128] + both[:, 128:256]
         for r in range(0, 64, 16):
             rows = slice(r, r + 16)
 
@@ -138,10 +157,10 @@
                 return total
 
             for c in range(5):
-                partly[c, z, rows, :] = state[c, z, rows, :] - step_size * (dx[c, rows, :] + along_y(c))
+                partly[c, z, rows, :] = state[c, z, rows, :] - step_size * (dx[c, z, rows, :] + along_y(c))
             curls[0, z, rows, :] = along_y(6)
-            curls[1, z, rows, :] = dx[6, rows, :]
-            curls[2, z, rows, :] = dx[5, rows, :] - along_y(5)
+            curls[1, z, rows, :] = dx[6, z, rows, :]
+            curls[2, z, rows, :] = dx[5, z, rows, :] - along_y(5)
         return 0
 
     lax.fori_loop(0, 8, plane, 0)
@@ -160,6 +179,14 @@
     return jnp.where(odd_slot, left, right), jnp.where(odd_slot, right, left)
 
 
+def edge_pairs(fields, x_low, x_high, from_left, from_right):
+    refs = (x_low, x_high, from_left, from_right)
+    return [
+        edge_corrections(high - left, right - low)
+        for low, high, left, right in zip(*[fields(lambda c, ref=ref: ref[c]) for ref in refs])
+    ]
+
+
 def edge_tile(corrections, chunk):
     lane = lax.broadcasted_iota(jnp.int32, (16, 128), 1)
     fix = turn(corrections[chunk % 2], -4 * (chunk - 1), 1)
@@ -168,7 +195,8 @@
 
 def render_kernel(
     ray_total,
-    pick,
+    grp,
+    index,
     flip,
     density_of,
     curls,
@@ -176,33 +204,42 @@
     x_high,
     from_left,
     from_right,
-    low_a,
-    high_a,
     below_a,
     above_a,
     tables,
-    segments,
+    sent,
     spins,
+    uv,
+    sems,
 ):
-    def crossing(ref):
-        inverse = 1.0 / ref[0]
-        return ref[2] * inverse, ref[3] * inverse
-
-    ours_low, ours_high, theirs_low, theirs_high = (
-        crossing(r) for r in (x_low, x_high, from_left, from_right)
-    )
-    v_edge, w_edge = (
-        edge_corrections(ours_high[n] - theirs_low[n], theirs_high[n] - ours_low[n]) for n in range(2)
-    )
-    blocks = (below_a, low_a, high_a, above_a)
-
+    copies = [
+        pltpu.make_async_copy(below_a, uv.at[:, 0:4], sems.at[0]),
+        pltpu.make_async_copy(above_a, uv.at[:, 12:16], sems.at[1]),
+    ]
+    for copy in copies:
+        copy.start()
+    edges_of = (x_low, x_high, from_left, from_right)
+    def own_plane(z, _):
+        for r in range(0, 64, 16):
+            rows = slice(r, r + 16)
+            inverse = 1.0 / density_of[0, z, rows, :]
+            uv[0, z + 4, rows, :] = density_of[1, z, rows, :] * inverse
+            uv[1, z + 4, rows, :] = density_of[2, z, rows, :] * inverse
+        return 0
+
+    lax.fori_loop(0, 8, own_plane, 0)
+    for copy in copies:
+        copy.wait()
+
+    def crossing(read):
+        inverse = 1.0 / read(0)
+        return read(2) * inverse, read(3) * inverse
+
+    v_edge, w_edge = edge_pairs(crossing, *edges_of)
     def depth(c, z, rows):
         total = None
         for k in range(4):
-            up, down = z + 5 + k, z + 3 - k
-            upper = blocks[up // 4][c, up % 4, rows, :]
-            lower = blocks[down // 4][c, down % 4, rows, :]
-            addend = weights[k] * (upper - lower)
+            addend = weights[k] * (uv[c, z + 5 + k, rows, :] - uv[c, z + 3 - k, rows, :])
             total = addend if k == 0 else total + addend
         return total
 
@@ -215,9 +252,13 @@
             third = curls[2, z, rows, :] + edge_tile(v_edge, chunk)
             spins[z, rows, :] = jnp.sqrt(first * first + second * second + third * third)
 
-    flipped = flip[...] == 1
+    lanes = lax.broadcasted_iota(jnp.int32, (8, 128), 1)
+    rows_of = lax.broadcasted_iota(jnp.int32, (8, 128), 0)
+    piece_lane = 16 * rows_of + 2 * (lanes & 7)
+    outgoing = jnp.zeros((8, 128), f32)
+    flipped = spread_flip(flip, lanes >> 1) == 1
     for i in range(4):
-        chosen = pick[i]
+        chosen = index[4 * grp[0] + i]
         halves = []
         for c in range(4):
             first = jnp.broadcast_to(tables[chosen, c : c + 1, 0:128], (8, 128))
@@ -244,13 +285,13 @@
             cell = jnp.minimum(coord.astype(jnp.int32), 255)
             part = coord - cell.astype(f32)
             low_half = cell < 128
-            index = cell & 127
+            entry = cell & 127
 
             def look(a, b):
                 return jnp.where(
                     low_half,
-                    jnp.take_along_axis(a, index, axis=1),
-                    jnp.take_along_axis(b, index, axis=1),
+                    jnp.take_along_axis(a, entry, axis=1),
+                    jnp.take_along_axis(b, entry, axis=1),
                 )
 
             entries = [look(h[0], h[1]) + part * look(h[2], h[3]) for h in halves]
@@ -260,11 +301,17 @@
         for span in (1, 2, 4):
             later = [turn(t, -span, 0) for t in total]
             total = joined(total, later, flipped)
-        lanes = lax.broadcasted_iota(jnp.int32, (8, 128), 1)
-        compact = (2 * lanes) & 127
         for c in range(4):
-            row = jnp.take_along_axis(total[c], compact, axis=1)
-            segments[4 * i + c : 4 * i + c + 1, :] = row[0:1, :]
+            row = jnp.broadcast_to(total[c][0:1, :], (8, 128))
+            row = jnp.take_along_axis(row, piece_lane, axis=1)
+            outgoing = jnp.where(lanes >> 3 == 4 * i + c, row, outgoing)
+    for g in range(4):
+        sent[8 * g : 8 * g + 8, :] = outgoing
+
+
+def spread_flip(flip, lane):
+    both = jnp.concatenate([flip[...], flip[...]], axis=1)
+    return jnp.take_along_axis(jnp.broadcast_to(both, lane.shape), lane, axis=1)
 
 
 def joined(near, far, flipped):
@@ -274,16 +321,8 @@
     return colors + [near[3] * far[3]]
 
 
-def depth_kernel(partly, state, x_low, x_high, from_left, from_right, out, fz):
-    def packed(ref):
-        rho, mx, my, mz, energy = (ref[c] for c in range(5))
-        return east_fields(mx, my, mz, energy, *primitives(rho, mx, my, mz, energy))[:5]
-
-    ours_low, ours_high = packed(x_low), packed(x_high)
-    theirs_low, theirs_high = packed(from_left), packed(from_right)
-    edges = [
-        edge_corrections(ours_high[n] - theirs_low[n], theirs_high[n] - ours_low[n]) for n in range(5)
-    ]
+def depth_kernel(partly, state, *refs):
+    edges_of, out, fz = refs[:4], refs[4], refs[5]
     for z in range(8):
         for r in range(0, 64, 16):
             rows = slice(r, r + 16)
@@ -291,6 +330,12 @@
             fields = up_fields(mz, energy, *primitives(rho, mx, my, mz, energy))
             for c in range(5):
                 fz[c, z, rows, :] = fields[c]
+
+    def packed(read):
+        rho, mx, my, mz, energy = (read(c) for c in range(5))
+        return east_fields(mx, my, mz, energy, *primitives(rho, mx, my, mz, energy))[:5]
+
+    edges = edge_pairs(packed, *edges_of)
     for c in range(5):
         for z in range(8):
             for b in range(4):
@@ -304,7 +349,20 @@
                 out[c, z, rows, :] = partly[c, z, rows, :] - step_size * total
 
 
-def last_kernel(partly, below_a, below_b, above_a, above_b, out, fz):
+def last_kernel(partly, *refs):
+    below_in, below_b, above_in, above_b, out, fz, held, below_a, above_a, sems, out_sems = refs
+    copies = [
+        pltpu.make_async_copy(below_in, below_a, sems.at[0]),
+        pltpu.make_async_copy(above_in, above_a, sems.at[1]),
+    ]
+    for copy in copies:
+        copy.start()
+    for copy in copies:
+        copy.wait()
+
+    def sending(c):
+        return pltpu.make_async_copy(held.at[c], out.at[c], out_sems.at[c])
+
     for side, (a, b) in enumerate(((below_a, below_b), (above_a, above_b))):
         for p in range(4):
             for r in range(0, 64, 16):
@@ -326,13 +384,17 @@
                         total = total - weights[k] * fz[c, 4 + z + k + 1 - 8, rows, :]
                     if z - k - 1 < 0:
                         total = total + weights[k] * fz[c, z - k - 1 + 4, rows, :]
-                out[c, z, rows, :] = total
-
-
-def compose_kernel(me, owner, flip, pieces, out):
+                held[c, z, rows, :] = total
+        sending(c).start()
+    for c in range(5):
+        sending(c).wait()
+
+
+def compose_kernel(me, depth, owner, flip, pieces, out):
     lane = lax.broadcasted_iota(jnp.int32, (4, 128), 1)
     channel = lane >> 3 & 3
-    flipped = flip[...] == 1
+    lanes = lax.broadcasted_iota(jnp.int32, (8, 128), 1)
+    flipped = spread_flip(flip, 8 * depth[0] + (lanes & 7))[0:4] == 1
 
     def passing(x):
         return jnp.where(
@@ -407,38 +469,47 @@
     partly, curls = pl.pallas_call(
         inner_kernel,
         out_shape=(shape(5, 8, 64, 128), shape(3, 8, 64, 128)),
-        in_specs=[VM] * 4,
+        in_specs=[VM, VM, VM],
         out_specs=(VM, VM),
         scratch_shapes=[
+            pltpu.VMEM((256, 256), jnp.bfloat16),
             pltpu.VMEM((7, 8, 80, 128), f32),
             pltpu.VMEM((7, 64, 256), jnp.bfloat16),
-            pltpu.VMEM((7, 64, 128), f32),
+            pltpu.VMEM((7, 8, 64, 128), f32),
         ],
+        compiler_params=params(12),
+        cost_estimate=weight(0.3),
+    )(state, from_south, from_north)
+
+    low_b, high_b = pl.pallas_call(
+        third_pack_kernel,
+        out_shape=(shape(3, 4, 64, 128), shape(3, 4, 64, 128)),
+        in_specs=[VM],
+        out_specs=(VM, VM),
         compiler_params=params(),
-        cost_estimate=weight(1),
-    )(state, from_south, from_north, jnp.asarray(circulant_matrix()))
-
-    late = after(state, from_above_a, from_below_a)
-    from_above_b = lax.ppermute(jnp.stack([late[c, :4] for c in (0, 3, 4)]), "grp", ring("grp", -1))
-    from_below_b = lax.ppermute(jnp.stack([late[c, 4:] for c in (0, 3, 4)]), "grp", ring("grp", 1))
-
-    pick = lax.dynamic_slice_in_dim(tf_index, grp * 4, 4)
-    flip = jnp.repeat(view_flip, 2)[None, :]
-    segments = pl.pallas_call(
+        cost_estimate=weight(0.3),
+    )(after(state, x_low))
+    low_b, high_b = lax.optimization_barrier((low_b, high_b, from_above_a, from_below_a))[:2]
+    from_above_b = lax.ppermute(low_b, "grp", ring("grp", -1))
+    from_below_b = lax.ppermute(high_b, "grp", ring("grp", 1))
+
+    flip = view_flip[None, :]
+    sent = pl.pallas_call(
         functools.partial(render_kernel, float(depth * 32)),
-        out_shape=shape(16, 128),
-        in_specs=[SM] + [VM] * 12,
+        out_shape=shape(32, 128),
+        in_specs=[SM] * 2 + [VM] * 7 + [HB] * 2 + [VM],
         out_specs=VM,
-        scratch_shapes=[pltpu.VMEM((8, 64, 128), f32)],
-        compiler_params=params(),
+        scratch_shapes=[
+            pltpu.VMEM((8, 64, 128), f32),
+            pltpu.VMEM((2, 16, 64, 128), f32),
+            pltpu.SemaphoreType.DMA((2,)),
+        ],
+        compiler_params=params(4),
         cost_estimate=weight(60),
     )(
-        pick, flip, state, curls, x_low, x_high, from_left, from_right,
-        low_a, high_a, from_below_a, from_above_a, tf_table,
+        grp[None], tf_index, flip, state, curls,
+        x_low, x_high, from_left, from_right, in_hbm(from_below_a), in_hbm(from_above_a), tf_table,
     )
-    width = 64 // depth
-    pieces = segments[:, :64].reshape(16, depth, width).transpose(1, 0, 2).reshape(depth, 16 * width)
-    sent = jnp.tile(pieces, (groups, 1))
     received = lax.all_to_all(sent, ("grp", "gy"), 0, 0, tiled=True).reshape(groups, depth, 128)
     most = pl.pallas_call(
         depth_kernel,
@@ -446,24 +517,30 @@
         in_specs=[VM] * 6,
         out_specs=VM,
         scratch_shapes=[pltpu.VMEM((5, 8, 64, 128), f32)],
-        compiler_params=params(),
-    )(after(partly, segments), state, x_low, x_high, from_left, from_right)
+        compiler_params=params(6),
+    )(after(partly, sent), state, x_low, x_high, from_left, from_right)
     new_state = pl.pallas_call(
         last_kernel,
         out_shape=shape(5, 8, 64, 128),
-        in_specs=[VM] * 5,
-        out_specs=VM,
-        scratch_shapes=[pltpu.VMEM((5, 8, 64, 128), f32)],
-        compiler_params=params(),
-    )(most, from_below_a, from_below_b, from_above_a, from_above_b)
-    own_flip = jnp.tile(lax.dynamic_slice_in_dim(view_flip, gy * width, width), 16)[None, :]
+        in_specs=[VM, HB, VM, HB, VM],
+        out_specs=HB,
+        scratch_shapes=[
+            pltpu.VMEM((5, 8, 64, 128), f32),
+            pltpu.VMEM((5, 8, 64, 128), f32),
+            pltpu.VMEM((2, 4, 64, 128), f32),
+            pltpu.VMEM((2, 4, 64, 128), f32),
+            pltpu.SemaphoreType.DMA((2,)),
+            pltpu.SemaphoreType.DMA((5,)),
+        ],
+        compiler_params=params(6),
+    )(most, in_hbm(from_below_a), from_below_b, in_hbm(from_above_a), from_above_b)
     image = pl.pallas_call(
         compose_kernel,
         out_shape=shape(8, 4, 8),
-        in_specs=[SM, SM, VM, VM],
+        in_specs=[SM, SM, SM, VM, VM],
         out_specs=VM,
         compiler_params=params(),
-    )(grp[None], owner[:, 0], own_flip, received)
+    )(grp[None], gy[None], owner[:, 0], flip, after(received, new_state))
     return (new_state, image)
 
 

time: 52.2 us -> 50 us (0.958)
  Pallas kernels: 9.51 us -> 14.7 us
  local copies, waits for them, and re-layouts: 6.73 us -> 1.93 us
  other arithmetic: 1.74 us -> 0 us
  starting transfers between devices: 28.7 us -> 28.1 us
    ppermute x1, starting transfers between devices: 6.1 us -> 0.08 us  [local(): from_left = lax.ppermute(x_high, 'gx', ring('gx', 1))]
    ppermute x1, starting transfers between devices: 4.06 us -> 8.55 us  [local(): from_right = lax.ppermute(x_low, 'gx', ring('gx', -1))]
    unnamed x30 -> x14, local copies, waits for them, and re-layouts: 5.34 us -> 1.93 us
    another operation x2 -> x0, other arithmetic: 1.74 us -> none  [the longest x1 0.97 us: local(): jnp.stack([late[c, 4:] for c in (0, 3, 4)])]
    pallas_call x1 -> x2, Pallas kernels: 1.52 us -> 3.25 us  [the longest x1 2.31 us: local(): pl.pallas_call(last_kernel, out_shape=shape(5, 8, 64, 128), in_specs=[VM,...]
    pallas_call x1, Pallas kernels: 2.74 us -> 4.14 us  [local(): pl.pallas_call(functools.partial(render_kernel, float(depth * 32)), out_s...]
    all_to_all x1, waiting for transfers between devices: 4.38 us -> 3.05 us  [local(): lax.all_to_all(sent, ('grp', 'gy'), 0, 0, tiled=True)]
    pallas_call x1, Pallas kernels: 2.4 us -> 3.61 us  [local(): pl.pallas_call(inner_kernel, out_shape=(shape(5, 8, 64, 128), shape(3, 8,...]
  transfers between devices with their start and end apart: 9 -> 9, of which waited for: 1 -> 2; matrix products, arithmetic and copies ran while one was open for 6% -> 0% of each run, Pallas kernels for 15% -> 27%
where the time goes in v1:
time: 50 us; the launch traced here: 49.7 us
  starting transfers between devices  28.1 us (56%)
  Pallas kernels  14.7 us (29%)
  waiting for transfers between devices  4.14 us (8%)
  local copies, waits for them, and re-layouts  1.93 us (4%)
  between operations  0.77 us (2%)
    all_to_all x1, starting transfers between devices, local(): lax.all_to_all(sent, ('grp', 'gy'), 0, 0, tiled=True)  8.78 us
    ppermute x1, starting transfers between devices, local(): from_right = lax.ppermute(x_low, 'gx', ring('gx', -1))  8.55 us
    pallas_call x1, Pallas kernels, local(): pl.pallas_call(functools.partial(render_kernel, float(depth * 32)), out_s...  4.14 us
    pallas_call x1, Pallas kernels, local(): pl.pallas_call(inner_kernel, out_shape=(shape(5, 8, 64, 128), shape(3, 8,...  3.61 us
    ppermute x1, starting transfers between devices, local(): from_above_b = lax.ppermute(low_b, 'grp', ring('grp', -1))  3.25 us
    all_to_all x1, waiting for transfers between devices, local(): lax.all_to_all(sent, ('grp', 'gy'), 0, 0, tiled=True)  3.05 us
    ppermute x1, starting transfers between devices, local(): from_above_a = lax.ppermute(low_a, 'grp', ring('grp', -1))  2.8 us
    ppermute x1, starting transfers between devices, local(): from_below_a = lax.ppermute(high_a, 'grp', ring('grp', 1))  2.54 us
  transfers between devices with their start and end apart: 9, of which 2 were waited for; matrix products, arithmetic and copies ran while one was open for 0% of the time, Pallas kernels for 27%

profile of v1, /device:TPU:1, one launch (start us, length us, event | category | flops | bytes accessed | tf_op | source)
XLA Modules:
  0.0 49.7 jit_solution(9234310958691684617)
XLA Ops:
  0.6 0.0 copy-start
  0.6 1.3 %copy-done = f32[5,8,64,128]{3,2,1,0:T(8,128)S(1)} copy-done((f32[5,8,64,128]{3,2,1,0:T(8,128)S(1)}, f32[5,8,64,128]{3,2,1,0:T(8,128)}, u32[]{:S(2)}) %copy-start) | copy-done | bytes 1310744
  1.9 0.1 shard_map.68
  2.0 2.5 %collective-permute-start.4 = (f32[2,4,64,128]{3,2,1,0:T(8,128)S(1)}, f32[2,4,64,128]{3,2,1,0:T(8,128)}, u32[]{:S(2)}, u32[]{:S(2)}) collective-permute-start(f32[2,4,64,128]{3,2,1,0:T(8,128)S(1)} %get-tuple-element.25), channel_id=1, source_target_pairs={{0,64},{64,128},{128,192},{192,0},{1,65},{65,129},{129,193},{193,1... | collective-permute-start | bytes 786440 | tf_op jit(solution)/shard_map/ppermute | solution.py:456
  4.6 2.8 %collective-permute-start.5 = (f32[2,4,64,128]{3,2,1,0:T(8,128)S(1)}, f32[2,4,64,128]{3,2,1,0:T(8,128)}, u32[]{:S(2)}, u32[]{:S(2)}) collective-permute-start(f32[2,4,64,128]{3,2,1,0:T(8,128)S(1)} %get-tuple-element.26), channel_id=1, source_target_pairs={{0,192},{64,0},{128,64},{192,128},{1,193},{65,1},{129,65},{193,129... | collective-permute-start | bytes 786440 | tf_op jit(solution)/shard_map/ppermute | solution.py:457
  7.4 1.8 %collective-permute-start.1 = (f32[5,4,8,128]{3,2,1,0:T(8,128)S(1)}, f32[5,4,8,128]{3,2,1,0:T(8,128)S(1)}, u32[]{:S(2)}, u32[]{:S(2)}) collective-permute-start(f32[5,4,8,128]{3,2,1,0:T(8,128)S(1)} %get-tuple-element.19), channel_id=1, source_target_pairs={{0,7},{1,0},{2,1},{3,2},{4,3},{5,4},{6,5},{7,6},{8,15},{9,8},{10,9... | collective-permute-start | bytes 245768 | tf_op jit(solution)/shard_map/ppermute | solution.py:459
  9.2 0.3 collective-permute-start
  9.4 0.4 shard_map.70
  9.8 8.5 %collective-permute-start.3 = (f32[5,16,128]{2,1,0:T(8,128)S(1)}, f32[5,16,128]{2,1,0:T(8,128)S(1)}, u32[]{:S(2)}, u32[]{:S(2)}) collective-permute-start(f32[5,16,128]{2,1,0:T(8,128)S(1)} %get-tuple-element.23.x_low.refs_0_), channel_id=1, source_target_pairs={{0,56},{8,0},{16,8},{24,16},{32,24},{40,32},{48,40},{56,48},{1,57}... | collective-permute-start | bytes 122888 | tf_op jit(solution)/shard_map/ppermute | solution.py:468
  18.4 0.1 collective-permute-start.2
  18.5 0.9 %shard_map.73 = (f32[3,4,64,128]{3,2,1,0:T(8,128)}, f32[3,4,64,128]{3,2,1,0:T(8,128)}) custom-call(f32[5,8,64,128]{3,2,1,0:T(8,128)S(1)} %copy-done), custom_call_target="tpu_custom_call" | custom-call | flops 300000000 | bytes 1000000 | tf_op jit(solution)/shard_map/pallas_call | solution.py:484
  19.4 3.6 %shard_map.69 = (f32[5,8,64,128]{3,2,1,0:T(8,128)S(1)}, f32[3,8,64,128]{3,2,1,0:T(8,128)S(1)}) custom-call(f32[5,8,64,128]{3,2,1,0:T(8,128)S(1)} %copy-done.1, f32[5,4,8,128]{3,2,1,0:T(8,128)S(1)} %collective-permute-done.from_south, f32[5,4,8,128]{3,2,1,0:T(8,128)S(1)} %collective-permute-done.1.from_north), custom_call_target="tpu_custom_call" | custom-call | flops 300000000 | bytes 1000000 | tf_op jit(solution)/shard_map/pallas_call | solution.py:469
  23.1 0.1 collective-permute-start.6
  23.1 3.3 %collective-permute-start.7 = (f32[3,4,64,128]{3,2,1,0:T(8,128)}, f32[3,4,64,128]{3,2,1,0:T(8,128)S(1)}, u32[]{:S(2)}, u32[]{:S(2)}) collective-permute-start(f32[3,4,64,128]{3,2,1,0:T(8,128)} %get-tuple-element.32), channel_id=1, source_target_pairs={{0,192},{64,0},{128,64},{192,128},{1,193},{65,1},{129,65},{193,129... | collective-permute-start | bytes 1179656 | tf_op jit(solution)/shard_map/ppermute | solution.py:493
  26.4 1.1 %collective-permute-done.2.from_left.refs_2_ = f32[5,16,128]{2,1,0:T(8,128)} collective-permute-done((f32[5,16,128]{2,1,0:T(8,128)S(1)}, f32[5,16,128]{2,1,0:T(8,128)}, u32[]{:S(2)}, u32[]{:S(2)}) %collective-permute-start.2) | collective-permute-done | bytes 40992 | tf_op jit(solution)/shard_map/ppermute | solution.py:467
  27.5 4.1 %shard_map.71 = f32[32,128]{1,0:T(8,128)S(1)} custom-call(s32[1]{0:T(128)} %bitcast.grp.me, s32[16]{0:T(128)S(1)} %copy-done.6, s32[1,64]{1,0:T(1,128)S(1)} %bitcast.11, f32[5,8,64,128]{3,2,1,0:T(8,128)S(1)} %copy-done.1, f32[3,8,64,128]{3,2,1,0:T(8,128)S(1)} %get-tuple-element.21.curls, f32[5,16,128]{2,1,0:T(8,128)S(1)} %get-tuple-element.23.x_low.refs_0_, ...), custom_call_target="tpu_custom_call" | custom-call | flops 60000002048 | bytes 1000000 | tf_op jit(solution)/shard_map/pallas_call | solution.py:497
  31.6 0.0 copy-start.2
  31.6 0.6 %copy-done.2 = f32[32,128]{1,0:T(8,128)} copy-done((f32[32,128]{1,0:T(8,128)}, f32[32,128]{1,0:T(8,128)S(1)}, u32[]{:S(2)}) %copy-start.2) | copy-done | bytes 16408
  32.2 8.8 %all-to-all-start = ((f32[32,1,128]{2,1,0:T(1,128)}), f32[32,1,128]{2,1,0:T(1,128)S(1)}, u32[]{:S(2)}, u32[]{:S(2)}) async-start(f32[32,1,128]{2,1,0:T(1,128)} %bitcast.9), calls=%async_computation | async-start | bytes 32768 | tf_op jit(solution)/shard_map/all_to_all | solution.py:513
  41.0 1.8 %shard_map.72.partly = f32[5,8,64,128]{3,2,1,0:T(8,128)S(1)} custom-call(f32[5,8,64,128]{3,2,1,0:T(8,128)S(1)} %get-tuple-element.27.partly, f32[5,8,64,128]{3,2,1,0:T(8,128)S(1)} %copy-done.1, f32[5,16,128]{2,1,0:T(8,128)S(1)} %get-tuple-element.23.x_low.refs_0_, f32[5,16,128]{2,1,0:T(8,128)S(1)} %get-tuple-element.24.x_high.refs_1_, ...), custom_call_target="tpu_custom_call" | custom-call | tf_op jit(solution)/shard_map/pallas_call | solution.py:514
  42.9 0.0 copy-start.3
  42.9 2.3 %shard_map.74 = f32[5,8,64,128]{3,2,1,0:T(8,128)} custom-call(f32[5,8,64,128]{3,2,1,0:T(8,128)S(1)} %shard_map.72.partly, f32[2,4,64,128]{3,2,1,0:T(8,128)} %collective-permute-done.4.below_a.refs_0_, f32[3,4,64,128]{3,2,1,0:T(8,128)S(1)} %collective-permute-done.6.refs_1_, f32[2,4,64,128]{3,2,1,0:T(8,128)} %collective-permute-done.5.above_a.refs_2_, ...), custom_call_target="tpu_custom_call" | custom-call | tf_op jit(solution)/shard_map/pallas_call | solution.py:522
  45.2 3.0 %all-to-all-done = f32[32,1,128]{2,1,0:T(1,128)S(1)} async-done(((f32[32,1,128]{2,1,0:T(1,128)}), f32[32,1,128]{2,1,0:T(1,128)S(1)}, u32[]{:S(2)}, u32[]{:S(2)}) %all-to-all-start) | async-done | bytes 16416 | tf_op jit(solution)/shard_map/all_to_all | solution.py:513
  48.3 1.5 %shard_map.75 = f32[8,4,8]{2,1,0:T(4,128)} custom-call(s32[1]{0:T(128)} %bitcast.grp.me, s32[1]{0:T(128)} %bitcast.2.depth, s32[16]{0:T(128)S(1)} %bitcast.10, s32[1,64]{1,0:T(1,128)S(1)} %bitcast.12, f32[4,8,128]{2,1,0:T(8,128)S(1)} %bitcast.8), custom_call_target="tpu_custom_call" | custom-call | tf_op jit(solution)/shard_map/pallas_call | solution.py:537
  (16 shorter events, 0.0 us)
Async XLA Ops:
  0.6 1.3 %copy-start = (f32[5,8,64,128]{3,2,1,0:T(8,128)S(1)}, f32[5,8,64,128]{3,2,1,0:T(8,128)}, u32[]{:S(2)}) copy-start(f32[5,8,64,128]{3,2,1,0:T(8,128)} %state.7) | copy-start | bytes 3932164
  2.0 21.0 %collective-permute-start.4 = (f32[2,4,64,128]{3,2,1,0:T(8,128)S(1)}, f32[2,4,64,128]{3,2,1,0:T(8,128)}, u32[]{:S(2)}, u32[]{:S(2)}) collective-permute-start(f32[2,4,64,128]{3,2,1,0:T(8,128)S(1)} %get-tuple-element.25), channel_id=1, source_target_pairs={{0,64},{64,128},{128,192},{192,0},{1,65},{65,129},{129,193},{193,1... | collective-permute-start | bytes 786440 | tf_op jit(solution)/shard_map/ppermute | solution.py:456
  4.6 18.5 %collective-permute-start.5 = (f32[2,4,64,128]{3,2,1,0:T(8,128)S(1)}, f32[2,4,64,128]{3,2,1,0:T(8,128)}, u32[]{:S(2)}, u32[]{:S(2)}) collective-permute-start(f32[2,4,64,128]{3,2,1,0:T(8,128)S(1)} %get-tuple-element.26), channel_id=1, source_target_pairs={{0,192},{64,0},{128,64},{192,128},{1,193},{65,1},{129,65},{193,129... | collective-permute-start | bytes 786440 | tf_op jit(solution)/shard_map/ppermute | solution.py:457
  7.4 11.0 %collective-permute-start.1 = (f32[5,4,8,128]{3,2,1,0:T(8,128)S(1)}, f32[5,4,8,128]{3,2,1,0:T(8,128)S(1)}, u32[]{:S(2)}, u32[]{:S(2)}) collective-permute-start(f32[5,4,8,128]{3,2,1,0:T(8,128)S(1)} %get-tuple-element.19), channel_id=1, source_target_pairs={{0,7},{1,0},{2,1},{3,2},{4,3},{5,4},{6,5},{7,6},{8,15},{9,8},{10,9... | collective-permute-start | bytes 245768 | tf_op jit(solution)/shard_map/ppermute | solution.py:459
  9.2 10.3 %copy-start.1 = (f32[5,8,64,128]{3,2,1,0:T(8,128)S(1)}, f32[5,8,64,128]{3,2,1,0:T(8,128)}, u32[]{:S(2)}) copy-start(f32[5,8,64,128]{3,2,1,0:T(8,128)} %state.7) | copy-start | bytes 3932164
  9.2 10.3 %collective-permute-start = (f32[5,4,8,128]{3,2,1,0:T(8,128)S(1)}, f32[5,4,8,128]{3,2,1,0:T(8,128)S(1)}, u32[]{:S(2)}, u32[]{:S(2)}) collective-permute-start(f32[5,4,8,128]{3,2,1,0:T(8,128)S(1)} %get-tuple-element.18), channel_id=1, source_target_pairs={{0,1},{1,2},{2,3},{3,4},{4,5},{5,6},{6,7},{7,0},{8,9},{9,10},{10,1... | collective-permute-start | bytes 245768 | tf_op jit(solution)/shard_map/ppermute | solution.py:458
  9.8 16.6 %collective-permute-start.3 = (f32[5,16,128]{2,1,0:T(8,128)S(1)}, f32[5,16,128]{2,1,0:T(8,128)S(1)}, u32[]{:S(2)}, u32[]{:S(2)}) collective-permute-start(f32[5,16,128]{2,1,0:T(8,128)S(1)} %get-tuple-element.23.x_low.refs_0_), channel_id=1, source_target_pairs={{0,56},{8,0},{16,8},{24,16},{32,24},{40,32},{48,40},{56,48},{1,57}... | collective-permute-start | bytes 122888 | tf_op jit(solution)/shard_map/ppermute | solution.py:468
  18.4 9.1 %copy-start.4 = (s32[64]{0:T(128)S(1)}, s32[64]{0:T(128)}, u32[]{:S(2)}) copy-start(s32[64]{0:T(128)} %param.9) | copy-start | bytes 772
  18.4 9.1 %copy-start.5 = (f32[4,4,256]{2,1,0:T(4,128)S(1)}, f32[4,4,256]{2,1,0:T(4,128)}, u32[]{:S(2)}) copy-start(f32[4,4,256]{2,1,0:T(4,128)} %tables.1) | copy-start | bytes 49156
  18.4 9.1 %copy-start.6 = (s32[16]{0:T(128)S(1)}, s32[16]{0:T(128)}, u32[]{:S(2)}) copy-start(s32[16]{0:T(128)} %index.1) | copy-start | bytes 196
  18.4 9.1 %collective-permute-start.2 = (f32[5,16,128]{2,1,0:T(8,128)S(1)}, f32[5,16,128]{2,1,0:T(8,128)}, u32[]{:S(2)}, u32[]{:S(2)}) collective-permute-start(f32[5,16,128]{2,1,0:T(8,128)S(1)} %get-tuple-element.24.x_high.refs_1_), channel_id=1, source_target_pairs={{0,8},{8,16},{16,24},{24,32},{32,40},{40,48},{48,56},{56,0},{1,9},... | collective-permute-start | bytes 122888 | tf_op jit(solution)/shard_map/ppermute | solution.py:467
  23.1 19.8 %collective-permute-start.6 = (f32[3,4,64,128]{3,2,1,0:T(8,128)}, f32[3,4,64,128]{3,2,1,0:T(8,128)S(1)}, u32[]{:S(2)}, u32[]{:S(2)}) collective-permute-start(f32[3,4,64,128]{3,2,1,0:T(8,128)} %get-tuple-element.31), channel_id=1, source_target_pairs={{0,64},{64,128},{128,192},{192,0},{1,65},{65,129},{129,193},{193,1... | collective-permute-start | bytes 1179656 | tf_op jit(solution)/shard_map/ppermute | solution.py:494
  23.1 19.7 %collective-permute-start.7 = (f32[3,4,64,128]{3,2,1,0:T(8,128)}, f32[3,4,64,128]{3,2,1,0:T(8,128)S(1)}, u32[]{:S(2)}, u32[]{:S(2)}) collective-permute-start(f32[3,4,64,128]{3,2,1,0:T(8,128)} %get-tuple-element.32), channel_id=1, source_target_pairs={{0,192},{64,0},{128,64},{192,128},{1,193},{65,1},{129,65},{193,129... | collective-permute-start | bytes 1179656 | tf_op jit(solution)/shard_map/ppermute | solution.py:493
  31.6 0.6 %copy-start.2 = (f32[32,128]{1,0:T(8,128)}, f32[32,128]{1,0:T(8,128)S(1)}, u32[]{:S(2)}) copy-start(f32[32,128]{1,0:T(8,128)S(1)} %shard_map.71) | copy-start | bytes 49156
  32.2 16.0 %all-to-all-start = ((f32[32,1,128]{2,1,0:T(1,128)}), f32[32,1,128]{2,1,0:T(1,128)S(1)}, u32[]{:S(2)}, u32[]{:S(2)}) async-start(f32[32,1,128]{2,1,0:T(1,128)} %bitcast.9), calls=%async_computation | async-start | bytes 32768 | tf_op jit(solution)/shard_map/all_to_all | solution.py:513
  42.9 5.4 %copy-start.3 = (s32[16,1]{0,1:T(1,128)S(1)}, s32[16,1]{0,1:T(1,128)}, u32[]{:S(2)}) copy-start(s32[16,1]{0,1:T(1,128)} %param.7) | copy-start | bytes 196

commit v2 on v1

--- a/solution.py
+++ b/solution.py
@@ -112,29 +112,8 @@
         matrix[half, 128:256] = low
 
 
-def inner_kernel(
-    state, from_south, from_north, partly, curls, matrix, yf, xf, dx
-):
+def inner_kernel(state, from_south, from_north, partly, curls, matrix, yf, xf, dx):
     write_circulant(matrix)
-
-    def fields_of(z, _):
-        for r in range(0, 64, 16):
-            rows = slice(r, r + 16)
-            rho, mx, my, mz, energy = (state[c, z, rows, :] for c in range(5))
-            parts = primitives(rho, mx, my, mz, energy)
-            north_parts = north_fields(mx, my, mz, energy, *parts)
-            east_parts = east_fields(mx, my, mz, energy, *parts)
-            for n in range(7):
-                yf[n, z, 8 + r : 24 + r, :] = north_parts[n]
-                high, low = split(east_parts[n])
-                xf[n, rows, 0:128] = high
-                xf[n, rows, 128:256] = low
-        for n in range(7):
-            both = jnp.dot(xf[n], matrix[...], preferred_element_type=f32)
-            dx[n, z] = both[:, 0:128] + both[:, 128:256]
-        return 0
-
-    lax.fori_loop(0, 8, fields_of, 0)
     for ref, base in ((from_south, 4), (from_north, 72)):
         for k in range(4):
             rho, mx, my, mz, energy = (ref[c, k] for c in range(5))
@@ -144,6 +123,20 @@
                 yf[n, 2 * k + 1, base : base + 4, :] = fields[n][4:8]
 
     def plane(z, _):
+        for r in range(0, 64, 16):
+            rows = slice(r, r + 16)
+            rho, mx, my, mz, energy = (state[c, z, rows, :] for c in range(5))
+            parts = primitives(rho, mx, my, mz, energy)
+            north = north_fields(mx, my, mz, energy, *parts)
+            east = east_fields(mx, my, mz, energy, *parts)
+            for n in range(7):
+                yf[n, z, 8 + r : 24 + r, :] = north[n]
+                high, low = split(east[n])
+                xf[n, rows, 0:128] = high
+                xf[n, rows, 128:256] = low
+        for n in range(7):
+            both = jnp.dot(xf[n], matrix[...], preferred_element_type=f32)
+            dx[n] = both[:, 0:128] + both[:, 128:256]
         for r in range(0, 64, 16):
             rows = slice(r, r + 16)
 
@@ -157,10 +150,10 @@
                 return total
 
             for c in range(5):
-                partly[c, z, rows, :] = state[c, z, rows, :] - step_size * (dx[c, z, rows, :] + along_y(c))
+                partly[c, z, rows, :] = state[c, z, rows, :] - step_size * (dx[c, rows, :] + along_y(c))
             curls[0, z, rows, :] = along_y(6)
-            curls[1, z, rows, :] = dx[6, z, rows, :]
-            curls[2, z, rows, :] = dx[5, z, rows, :] - along_y(5)
+            curls[1, z, rows, :] = dx[6, rows, :]
+            curls[2, z, rows, :] = dx[5, rows, :] - along_y(5)
         return 0
 
     lax.fori_loop(0, 8, plane, 0)
@@ -202,19 +195,24 @@
     curls,
     x_low,
     x_high,
-    from_left,
-    from_right,
+    left_in,
+    right_in,
     below_a,
     above_a,
     tables,
     sent,
     spins,
     uv,
+    looked,
+    from_left,
+    from_right,
     sems,
 ):
     copies = [
         pltpu.make_async_copy(below_a, uv.at[:, 0:4], sems.at[0]),
         pltpu.make_async_copy(above_a, uv.at[:, 12:16], sems.at[1]),
+        pltpu.make_async_copy(left_in, from_left, sems.at[2]),
+        pltpu.make_async_copy(right_in, from_right, sems.at[3]),
     ]
     for copy in copies:
         copy.start()
@@ -228,35 +226,15 @@
         return 0
 
     lax.fori_loop(0, 8, own_plane, 0)
-    for copy in copies:
-        copy.wait()
-
-    def crossing(read):
-        inverse = 1.0 / read(0)
-        return read(2) * inverse, read(3) * inverse
-
-    v_edge, w_edge = edge_pairs(crossing, *edges_of)
-    def depth(c, z, rows):
-        total = None
-        for k in range(4):
-            addend = weights[k] * (uv[c, z + 5 + k, rows, :] - uv[c, z + 3 - k, rows, :])
-            total = addend if k == 0 else total + addend
-        return total
-
-    for z in range(8):
-        for b in range(4):
-            rows = slice(16 * b, 16 * b + 16)
-            chunk = 4 * z + b
-            first = curls[0, z, rows, :] - depth(1, z, rows)
-            second = depth(0, z, rows) - (curls[1, z, rows, :] + edge_tile(w_edge, chunk))
-            third = curls[2, z, rows, :] + edge_tile(v_edge, chunk)
-            spins[z, rows, :] = jnp.sqrt(first * first + second * second + third * third)
-
-    lanes = lax.broadcasted_iota(jnp.int32, (8, 128), 1)
-    rows_of = lax.broadcasted_iota(jnp.int32, (8, 128), 0)
-    piece_lane = 16 * rows_of + 2 * (lanes & 7)
-    outgoing = jnp.zeros((8, 128), f32)
-    flipped = spread_flip(flip, lanes >> 1) == 1
+
+    def coarse(read, i, m):
+        gathered = None
+        for dz in range(2):
+            for dy in range(2):
+                part = read(2 * i + dz, pl.ds(2 * m + dy, 8, stride=8))
+                gathered = part if gathered is None else gathered + part
+        return (gathered + turn(gathered, -1, 1)) * 0.125
+
     for i in range(4):
         chosen = index[4 * grp[0] + i]
         halves = []
@@ -267,20 +245,8 @@
             after_first = jnp.where(last, turn(second, -1, 1), turn(first, -1, 1))
             after_second = jnp.where(last, second, turn(second, -1, 1))
             halves.append((first, second, after_first - first, after_second - second))
-
-        total = None
         for m in range(4):
-
-            def coarse(read):
-                gathered = None
-                for dz in range(2):
-                    for dy in range(2):
-                        part = read(2 * i + dz, pl.ds(2 * m + dy, 8, stride=8))
-                        gathered = part if gathered is None else gathered + part
-                return (gathered + turn(gathered, -1, 1)) * 0.125
-
-            density = coarse(lambda z, rows: density_of[0, z, rows, :])
-            spin = coarse(lambda z, rows: spins[z, rows, :])
+            density = coarse(lambda z, rows: density_of[0, z, rows, :], i, m)
             coord = 255.0 * jnp.clip((density - 0.9) / 0.6, 0.0, 1.0)
             cell = jnp.minimum(coord.astype(jnp.int32), 255)
             part = coord - cell.astype(f32)
@@ -294,7 +260,46 @@
                     jnp.take_along_axis(b, entry, axis=1),
                 )
 
-            entries = [look(h[0], h[1]) + part * look(h[2], h[3]) for h in halves]
+            for c, h in enumerate(halves):
+                looked[i, m, c] = look(h[0], h[1]) + part * look(h[2], h[3])
+
+    for copy in copies[2:]:
+        copy.wait()
+
+    def crossing(read):
+        inverse = 1.0 / read(0)
+        return read(2) * inverse, read(3) * inverse
+
+    v_edge, w_edge = edge_pairs(crossing, *edges_of)
+    for copy in copies[:2]:
+        copy.wait()
+
+    def depth(c, z, rows):
+        total = None
+        for k in range(4):
+            addend = weights[k] * (uv[c, z + 5 + k, rows, :] - uv[c, z + 3 - k, rows, :])
+            total = addend if k == 0 else total + addend
+        return total
+
+    for z in range(8):
+        for b in range(4):
+            rows = slice(16 * b, 16 * b + 16)
+            chunk = 4 * z + b
+            first = curls[0, z, rows, :] - depth(1, z, rows)
+            second = depth(0, z, rows) - (curls[1, z, rows, :] + edge_tile(w_edge, chunk))
+            third = curls[2, z, rows, :] + edge_tile(v_edge, chunk)
+            spins[z, rows, :] = jnp.sqrt(first * first + second * second + third * third)
+
+    lanes = lax.broadcasted_iota(jnp.int32, (8, 128), 1)
+    rows_of = lax.broadcasted_iota(jnp.int32, (8, 128), 0)
+    piece_lane = 16 * rows_of + 2 * (lanes & 7)
+    outgoing = jnp.zeros((8, 128), f32)
+    flipped = spread_flip(flip, lanes >> 1) == 1
+    for i in range(4):
+        total = None
+        for m in range(4):
+            spin = coarse(lambda z, rows: spins[z, rows, :], i, m)
+            entries = [looked[i, m, c] for c in range(4)]
             opacity = opacity_gain * entries[3] * spin / (1.0 + spin) / ray_total
             piece = [entries[c] * opacity for c in range(3)] + [1.0 - opacity]
             total = piece if total is None else joined(total, piece, flipped)
@@ -475,7 +480,7 @@
             pltpu.VMEM((256, 256), jnp.bfloat16),
             pltpu.VMEM((7, 8, 80, 128), f32),
             pltpu.VMEM((7, 64, 256), jnp.bfloat16),
-            pltpu.VMEM((7, 8, 64, 128), f32),
+            pltpu.VMEM((7, 64, 128), f32),
         ],
         compiler_params=params(12),
         cost_estimate=weight(0.3),
@@ -497,12 +502,15 @@
     sent = pl.pallas_call(
         functools.partial(render_kernel, float(depth * 32)),
         out_shape=shape(32, 128),
-        in_specs=[SM] * 2 + [VM] * 7 + [HB] * 2 + [VM],
+        in_specs=[SM] * 2 + [VM] * 5 + [HB] * 4 + [VM],
         out_specs=VM,
         scratch_shapes=[
             pltpu.VMEM((8, 64, 128), f32),
             pltpu.VMEM((2, 16, 64, 128), f32),
-            pltpu.SemaphoreType.DMA((2,)),
+            pltpu.VMEM((4, 4, 4, 8, 128), f32),
+            pltpu.VMEM((5, 16, 128), f32),
+            pltpu.VMEM((5, 16, 128), f32),
+            pltpu.SemaphoreType.DMA((4,)),
         ],
         compiler_params=params(4),
         cost_estimate=weight(60),

time: 50 us -> 48.7 us (0.974)
  Pallas kernels: 14.7 us -> 12.3 us
  waiting for transfers between devices: 4.14 us -> 5.3 us
    pallas_call x1, Pallas kernels: 4.14 us -> 2.85 us  [local(): pl.pallas_call(functools.partial(render_kernel, float(depth * 32)), out_s...]
    ppermute x1, waiting for transfers between devices: 1.07 us -> 2.23 us  [local(): from_left = lax.ppermute(x_high, 'gx', ring('gx', 1))]
    pallas_call x1, Pallas kernels: 3.61 us -> 2.45 us  [local(): pl.pallas_call(inner_kernel, out_shape=(shape(5, 8, 64, 128), shape(3, 8,...]
  transfers between devices with their start and end apart: 9 -> 9, of which waited for: 2 -> 2; matrix products, arithmetic and copies ran while one was open for 0% -> 0% of each run, Pallas kernels for 27% -> 22%
where the time goes in v2:
time: 48.7 us; the launch traced here: 48.4 us
  starting transfers between devices  28.2 us (58%)
  Pallas kernels  12.3 us (25%)
  waiting for transfers between devices  5.3 us (11%)
  local copies, waits for them, and re-layouts  1.93 us (4%)
  between operations  0.76 us (2%)
    all_to_all x1, starting transfers between devices, local(): lax.all_to_all(sent, ('grp', 'gy'), 0, 0, tiled=True)  8.79 us
    ppermute x1, starting transfers between devices, local(): from_right = lax.ppermute(x_low, 'gx', ring('gx', -1))  8.55 us
    ppermute x1, starting transfers between devices, local(): from_above_b = lax.ppermute(low_b, 'grp', ring('grp', -1))  3.25 us
    all_to_all x1, waiting for transfers between devices, local(): lax.all_to_all(sent, ('grp', 'gy'), 0, 0, tiled=True)  3.05 us
    pallas_call x1, Pallas kernels, local(): pl.pallas_call(functools.partial(render_kernel, float(depth * 32)), out_s...  2.85 us
    ppermute x1, starting transfers between devices, local(): from_above_a = lax.ppermute(low_a, 'grp', ring('grp', -1))  2.8 us
    ppermute x1, starting transfers between devices, local(): from_below_a = lax.ppermute(high_a, 'grp', ring('grp', 1))  2.54 us
    pallas_call x1, Pallas kernels, local(): pl.pallas_call(inner_kernel, out_shape=(shape(5, 8, 64, 128), shape(3, 8,...  2.45 us
  transfers between devices with their start and end apart: 9, of which 2 were waited for; matrix products, arithmetic and copies ran while one was open for 0% of the time, Pallas kernels for 22%

profile of v2, /device:TPU:1, one launch (start us, length us, event | category | flops | bytes accessed | tf_op | source)
XLA Modules:
  0.0 48.4 jit_solution(7296045143205548429)
XLA Ops:
  0.6 0.0 copy-start
  0.6 1.3 %copy-done = f32[5,8,64,128]{3,2,1,0:T(8,128)S(1)} copy-done((f32[5,8,64,128]{3,2,1,0:T(8,128)S(1)}, f32[5,8,64,128]{3,2,1,0:T(8,128)}, u32[]{:S(2)}) %copy-start) | copy-done | bytes 1310744
  1.9 0.1 shard_map.68
  2.0 2.5 %collective-permute-start.4 = (f32[2,4,64,128]{3,2,1,0:T(8,128)S(1)}, f32[2,4,64,128]{3,2,1,0:T(8,128)}, u32[]{:S(2)}, u32[]{:S(2)}) collective-permute-start(f32[2,4,64,128]{3,2,1,0:T(8,128)S(1)} %get-tuple-element.25), channel_id=1, source_target_pairs={{0,64},{64,128},{128,192},{192,0},{1,65},{65,129},{129,193},{193,1... | collective-permute-start | bytes 786440 | tf_op jit(solution)/shard_map/ppermute | solution.py:461
  4.6 2.8 %collective-permute-start.5 = (f32[2,4,64,128]{3,2,1,0:T(8,128)S(1)}, f32[2,4,64,128]{3,2,1,0:T(8,128)}, u32[]{:S(2)}, u32[]{:S(2)}) collective-permute-start(f32[2,4,64,128]{3,2,1,0:T(8,128)S(1)} %get-tuple-element.26), channel_id=1, source_target_pairs={{0,192},{64,0},{128,64},{192,128},{1,193},{65,1},{129,65},{193,129... | collective-permute-start | bytes 786440 | tf_op jit(solution)/shard_map/ppermute | solution.py:462
  7.4 1.8 %collective-permute-start.1 = (f32[5,4,8,128]{3,2,1,0:T(8,128)S(1)}, f32[5,4,8,128]{3,2,1,0:T(8,128)S(1)}, u32[]{:S(2)}, u32[]{:S(2)}) collective-permute-start(f32[5,4,8,128]{3,2,1,0:T(8,128)S(1)} %get-tuple-element.19), channel_id=1, source_target_pairs={{0,7},{1,0},{2,1},{3,2},{4,3},{5,4},{6,5},{7,6},{8,15},{9,8},{10,9... | collective-permute-start | bytes 245768 | tf_op jit(solution)/shard_map/ppermute | solution.py:464
  9.2 0.3 collective-permute-start
  9.4 0.4 shard_map.70
  9.8 8.5 %collective-permute-start.3 = (f32[5,16,128]{2,1,0:T(8,128)S(1)}, f32[5,16,128]{2,1,0:T(8,128)S(1)}, u32[]{:S(2)}, u32[]{:S(2)}) collective-permute-start(f32[5,16,128]{2,1,0:T(8,128)S(1)} %get-tuple-element.23.x_low.refs_0_), channel_id=1, source_target_pairs={{0,56},{8,0},{16,8},{24,16},{32,24},{40,32},{48,40},{56,48},{1,57}... | collective-permute-start | bytes 122888 | tf_op jit(solution)/shard_map/ppermute | solution.py:473
  18.4 0.1 collective-permute-start.2
  18.5 0.9 %shard_map.73 = (f32[3,4,64,128]{3,2,1,0:T(8,128)}, f32[3,4,64,128]{3,2,1,0:T(8,128)}) custom-call(f32[5,8,64,128]{3,2,1,0:T(8,128)S(1)} %copy-done), custom_call_target="tpu_custom_call" | custom-call | flops 300000000 | bytes 1000000 | tf_op jit(solution)/shard_map/pallas_call | solution.py:489
  19.4 2.4 %shard_map.69 = (f32[5,8,64,128]{3,2,1,0:T(8,128)S(1)}, f32[3,8,64,128]{3,2,1,0:T(8,128)S(1)}) custom-call(f32[5,8,64,128]{3,2,1,0:T(8,128)S(1)} %copy-done.1, f32[5,4,8,128]{3,2,1,0:T(8,128)S(1)} %collective-permute-done.from_south, f32[5,4,8,128]{3,2,1,0:T(8,128)S(1)} %collective-permute-done.1.from_north), custom_call_target="tpu_custom_call" | custom-call | flops 300000000 | bytes 1000000 | tf_op jit(solution)/shard_map/pallas_call | solution.py:474
  21.9 0.1 collective-permute-start.6
  22.0 3.3 %collective-permute-start.7 = (f32[3,4,64,128]{3,2,1,0:T(8,128)}, f32[3,4,64,128]{3,2,1,0:T(8,128)S(1)}, u32[]{:S(2)}, u32[]{:S(2)}) collective-permute-start(f32[3,4,64,128]{3,2,1,0:T(8,128)} %get-tuple-element.32), channel_id=1, source_target_pairs={{0,192},{64,0},{128,64},{192,128},{1,193},{65,1},{129,65},{193,129... | collective-permute-start | bytes 1179656 | tf_op jit(solution)/shard_map/ppermute | solution.py:498
  25.2 2.2 %collective-permute-done.2.left_in.refs_2_ = f32[5,16,128]{2,1,0:T(8,128)} collective-permute-done((f32[5,16,128]{2,1,0:T(8,128)S(1)}, f32[5,16,128]{2,1,0:T(8,128)}, u32[]{:S(2)}, u32[]{:S(2)}) %collective-permute-start.2) | collective-permute-done | bytes 40992 | tf_op jit(solution)/shard_map/ppermute | solution.py:472
  27.5 2.8 %shard_map.71 = f32[32,128]{1,0:T(8,128)S(1)} custom-call(s32[1]{0:T(128)} %bitcast.grp.me, s32[16]{0:T(128)S(1)} %copy-done.6, s32[1,64]{1,0:T(1,128)S(1)} %bitcast.11, f32[5,8,64,128]{3,2,1,0:T(8,128)S(1)} %copy-done.1, f32[3,8,64,128]{3,2,1,0:T(8,128)S(1)} %get-tuple-element.21.curls, f32[5,16,128]{2,1,0:T(8,128)S(1)} %get-tuple-element.23.x_low.refs_0_, ...), custom_call_target="tpu_custom_call" | custom-call | flops 60000002048 | bytes 1000000 | tf_op jit(solution)/shard_map/pallas_call | solution.py:502
  30.3 0.0 copy-start.2
  30.3 0.6 %copy-done.2 = f32[32,128]{1,0:T(8,128)} copy-done((f32[32,128]{1,0:T(8,128)}, f32[32,128]{1,0:T(8,128)S(1)}, u32[]{:S(2)}) %copy-start.2) | copy-done | bytes 16408
  30.9 8.8 %all-to-all-start = ((f32[32,1,128]{2,1,0:T(1,128)}), f32[32,1,128]{2,1,0:T(1,128)S(1)}, u32[]{:S(2)}, u32[]{:S(2)}) async-start(f32[32,1,128]{2,1,0:T(1,128)} %bitcast.9), calls=%async_computation | async-start | bytes 32768 | tf_op jit(solution)/shard_map/all_to_all | solution.py:521
  39.7 1.8 %shard_map.72.partly = f32[5,8,64,128]{3,2,1,0:T(8,128)S(1)} custom-call(f32[5,8,64,128]{3,2,1,0:T(8,128)S(1)} %get-tuple-element.27.partly, f32[5,8,64,128]{3,2,1,0:T(8,128)S(1)} %copy-done.1, f32[5,16,128]{2,1,0:T(8,128)S(1)} %get-tuple-element.23.x_low.refs_0_, f32[5,16,128]{2,1,0:T(8,128)S(1)} %get-tuple-element.24.x_high.refs_1_, ...), custom_call_target="tpu_custom_call" | custom-call | tf_op jit(solution)/shard_map/pallas_call | solution.py:522
  41.6 0.0 copy-start.3
  41.6 2.3 %shard_map.74 = f32[5,8,64,128]{3,2,1,0:T(8,128)} custom-call(f32[5,8,64,128]{3,2,1,0:T(8,128)S(1)} %shard_map.72.partly, f32[2,4,64,128]{3,2,1,0:T(8,128)} %collective-permute-done.4.below_a.refs_0_, f32[3,4,64,128]{3,2,1,0:T(8,128)S(1)} %collective-permute-done.6.refs_1_, f32[2,4,64,128]{3,2,1,0:T(8,128)} %collective-permute-done.5.above_a.refs_2_, ...), custom_call_target="tpu_custom_call" | custom-call | tf_op jit(solution)/shard_map/pallas_call | solution.py:530
  43.9 3.0 %all-to-all-done = f32[32,1,128]{2,1,0:T(1,128)S(1)} async-done(((f32[32,1,128]{2,1,0:T(1,128)}), f32[32,1,128]{2,1,0:T(1,128)S(1)}, u32[]{:S(2)}, u32[]{:S(2)}) %all-to-all-start) | async-done | bytes 16416 | tf_op jit(solution)/shard_map/all_to_all | solution.py:521
  47.0 1.5 %shard_map.75 = f32[8,4,8]{2,1,0:T(4,128)} custom-call(s32[1]{0:T(128)} %bitcast.grp.me, s32[1]{0:T(128)} %bitcast.2.depth, s32[16]{0:T(128)S(1)} %bitcast.10, s32[1,64]{1,0:T(1,128)S(1)} %bitcast.12, f32[4,8,128]{2,1,0:T(8,128)S(1)} %bitcast.8), custom_call_target="tpu_custom_call" | custom-call | tf_op jit(solution)/shard_map/pallas_call | solution.py:545
  (16 shorter events, 0.0 us)
Async XLA Ops:
  0.6 1.3 %copy-start = (f32[5,8,64,128]{3,2,1,0:T(8,128)S(1)}, f32[5,8,64,128]{3,2,1,0:T(8,128)}, u32[]{:S(2)}) copy-start(f32[5,8,64,128]{3,2,1,0:T(8,128)} %state.7) | copy-start | bytes 3932164
  2.0 19.9 %collective-permute-start.4 = (f32[2,4,64,128]{3,2,1,0:T(8,128)S(1)}, f32[2,4,64,128]{3,2,1,0:T(8,128)}, u32[]{:S(2)}, u32[]{:S(2)}) collective-permute-start(f32[2,4,64,128]{3,2,1,0:T(8,128)S(1)} %get-tuple-element.25), channel_id=1, source_target_pairs={{0,64},{64,128},{128,192},{192,0},{1,65},{65,129},{129,193},{193,1... | collective-permute-start | bytes 786440 | tf_op jit(solution)/shard_map/ppermute | solution.py:461
  4.6 17.3 %collective-permute-start.5 = (f32[2,4,64,128]{3,2,1,0:T(8,128)S(1)}, f32[2,4,64,128]{3,2,1,0:T(8,128)}, u32[]{:S(2)}, u32[]{:S(2)}) collective-permute-start(f32[2,4,64,128]{3,2,1,0:T(8,128)S(1)} %get-tuple-element.26), channel_id=1, source_target_pairs={{0,192},{64,0},{128,64},{192,128},{1,193},{65,1},{129,65},{193,129... | collective-permute-start | bytes 786440 | tf_op jit(solution)/shard_map/ppermute | solution.py:462
  7.4 11.0 %collective-permute-start.1 = (f32[5,4,8,128]{3,2,1,0:T(8,128)S(1)}, f32[5,4,8,128]{3,2,1,0:T(8,128)S(1)}, u32[]{:S(2)}, u32[]{:S(2)}) collective-permute-start(f32[5,4,8,128]{3,2,1,0:T(8,128)S(1)} %get-tuple-element.19), channel_id=1, source_target_pairs={{0,7},{1,0},{2,1},{3,2},{4,3},{5,4},{6,5},{7,6},{8,15},{9,8},{10,9... | collective-permute-start | bytes 245768 | tf_op jit(solution)/shard_map/ppermute | solution.py:464
  9.2 10.3 %copy-start.1 = (f32[5,8,64,128]{3,2,1,0:T(8,128)S(1)}, f32[5,8,64,128]{3,2,1,0:T(8,128)}, u32[]{:S(2)}) copy-start(f32[5,8,64,128]{3,2,1,0:T(8,128)} %state.7) | copy-start | bytes 3932164
  9.2 10.3 %collective-permute-start = (f32[5,4,8,128]{3,2,1,0:T(8,128)S(1)}, f32[5,4,8,128]{3,2,1,0:T(8,128)S(1)}, u32[]{:S(2)}, u32[]{:S(2)}) collective-permute-start(f32[5,4,8,128]{3,2,1,0:T(8,128)S(1)} %get-tuple-element.18), channel_id=1, source_target_pairs={{0,1},{1,2},{2,3},{3,4},{4,5},{5,6},{6,7},{7,0},{8,9},{9,10},{10,1... | collective-permute-start | bytes 245768 | tf_op jit(solution)/shard_map/ppermute | solution.py:463
  9.8 15.4 %collective-permute-start.3 = (f32[5,16,128]{2,1,0:T(8,128)S(1)}, f32[5,16,128]{2,1,0:T(8,128)S(1)}, u32[]{:S(2)}, u32[]{:S(2)}) collective-permute-start(f32[5,16,128]{2,1,0:T(8,128)S(1)} %get-tuple-element.23.x_low.refs_0_), channel_id=1, source_target_pairs={{0,56},{8,0},{16,8},{24,16},{32,24},{40,32},{48,40},{56,48},{1,57}... | collective-permute-start | bytes 122888 | tf_op jit(solution)/shard_map/ppermute | solution.py:473
  18.4 9.1 %copy-start.4 = (s32[64]{0:T(128)S(1)}, s32[64]{0:T(128)}, u32[]{:S(2)}) copy-start(s32[64]{0:T(128)} %param.9) | copy-start | bytes 772
  18.4 9.1 %copy-start.5 = (f32[4,4,256]{2,1,0:T(4,128)S(1)}, f32[4,4,256]{2,1,0:T(4,128)}, u32[]{:S(2)}) copy-start(f32[4,4,256]{2,1,0:T(4,128)} %tables.1) | copy-start | bytes 49156
  18.4 9.1 %copy-start.6 = (s32[16]{0:T(128)S(1)}, s32[16]{0:T(128)}, u32[]{:S(2)}) copy-start(s32[16]{0:T(128)} %index.1) | copy-start | bytes 196
  18.4 9.1 %collective-permute-start.2 = (f32[5,16,128]{2,1,0:T(8,128)S(1)}, f32[5,16,128]{2,1,0:T(8,128)}, u32[]{:S(2)}, u32[]{:S(2)}) collective-permute-start(f32[5,16,128]{2,1,0:T(8,128)S(1)} %get-tuple-element.24.x_high.refs_1_), channel_id=1, source_target_pairs={{0,8},{8,16},{16,24},{24,32},{32,40},{40,48},{48,56},{56,0},{1,9},... | collective-permute-start | bytes 122888 | tf_op jit(solution)/shard_map/ppermute | solution.py:472
  21.9 19.7 %collective-permute-start.6 = (f32[3,4,64,128]{3,2,1,0:T(8,128)}, f32[3,4,64,128]{3,2,1,0:T(8,128)S(1)}, u32[]{:S(2)}, u32[]{:S(2)}) collective-permute-start(f32[3,4,64,128]{3,2,1,0:T(8,128)} %get-tuple-element.31), channel_id=1, source_target_pairs={{0,64},{64,128},{128,192},{192,0},{1,65},{65,129},{129,193},{193,1... | collective-permute-start | bytes 1179656 | tf_op jit(solution)/shard_map/ppermute | solution.py:499
  22.0 19.6 %collective-permute-start.7 = (f32[3,4,64,128]{3,2,1,0:T(8,128)}, f32[3,4,64,128]{3,2,1,0:T(8,128)S(1)}, u32[]{:S(2)}, u32[]{:S(2)}) collective-permute-start(f32[3,4,64,128]{3,2,1,0:T(8,128)} %get-tuple-element.32), channel_id=1, source_target_pairs={{0,192},{64,0},{128,64},{192,128},{1,193},{65,1},{129,65},{193,129... | collective-permute-start | bytes 1179656 | tf_op jit(solution)/shard_map/ppermute | solution.py:498
  30.3 0.6 %copy-start.2 = (f32[32,128]{1,0:T(8,128)}, f32[32,128]{1,0:T(8,128)S(1)}, u32[]{:S(2)}) copy-start(f32[32,128]{1,0:T(8,128)S(1)} %shard_map.71) | copy-start | bytes 49156
  30.9 16.0 %all-to-all-start = ((f32[32,1,128]{2,1,0:T(1,128)}), f32[32,1,128]{2,1,0:T(1,128)S(1)}, u32[]{:S(2)}, u32[]{:S(2)}) async-start(f32[32,1,128]{2,1,0:T(1,128)} %bitcast.9), calls=%async_computation | async-start | bytes 32768 | tf_op jit(solution)/shard_map/all_to_all | solution.py:521
  41.6 5.4 %copy-start.3 = (s32[16,1]{0,1:T(1,128)S(1)}, s32[16,1]{0,1:T(1,128)}, u32[]{:S(2)}) copy-start(s32[16,1]{0,1:T(1,128)} %param.7) | copy-start | bytes 196

commit v3 on v2

--- a/solution.py
+++ b/solution.py
@@ -310,8 +310,7 @@
             row = jnp.broadcast_to(total[c][0:1, :], (8, 128))
             row = jnp.take_along_axis(row, piece_lane, axis=1)
             outgoing = jnp.where(lanes >> 3 == 4 * i + c, row, outgoing)
-    for g in range(4):
-        sent[8 * g : 8 * g + 8, :] = outgoing
+    sent[...] = outgoing
 
 
 def spread_flip(flip, lane):
@@ -395,31 +394,32 @@
         sending(c).wait()
 
 
-def compose_kernel(me, depth, owner, flip, pieces, out):
-    lane = lax.broadcasted_iota(jnp.int32, (4, 128), 1)
+def compose_kernel(depth, flip, pieces, out):
+    lane = lax.broadcasted_iota(jnp.int32, (8, 128), 1)[0:1]
     channel = lane >> 3 & 3
     lanes = lax.broadcasted_iota(jnp.int32, (8, 128), 1)
-    flipped = spread_flip(flip, 8 * depth[0] + (lanes & 7))[0:4] == 1
+    flipped = spread_flip(flip, 8 * depth[0] + (lanes & 7))[0:1] == 1
 
     def passing(x):
-        return jnp.where(
-            channel == 3,
-            x,
-            jnp.where(
-                channel == 2, turn(x, -8, 1), jnp.where(channel == 1, turn(x, -16, 1), turn(x, -24, 1))
-            ),
-        )
-
-    total = pieces[:, 0, :]
+        second = jnp.where(channel == 1, turn(x, -16, 1), turn(x, -24, 1))
+        return jnp.where(channel == 3, x, jnp.where(channel == 2, turn(x, -8, 1), second))
+
+    total = pieces[0:1, :]
     total_pass = passing(total)
     for j in range(1, 8):
-        later = pieces[:, j, :]
+        later = pieces[j : j + 1, :]
         later_pass = passing(later)
         both = total_pass * later_pass
         color = jnp.where(flipped, later + later_pass * total, total + total_pass * later)
         total = jnp.where(channel == 3, both, color)
         total_pass = both
-    total = jnp.where(channel == 3, 1.0 - total, total)
+    out[...] = jnp.where(channel == 3, 1.0 - total, total)
+
+
+def slot_kernel(me, owner, own, first, second, third, out, rows):
+    for k, ref in enumerate((own, first, second, third)):
+        rows[pl.ds((me[0] - k) & 3, 1), :] = ref[...]
+    total = rows[...]
     sub = lax.broadcasted_iota(jnp.int32, (8, 128), 0)
     result = jnp.zeros((8, 128), f32)
     count = jnp.int32(0)
@@ -501,7 +501,7 @@
     flip = view_flip[None, :]
     sent = pl.pallas_call(
         functools.partial(render_kernel, float(depth * 32)),
-        out_shape=shape(32, 128),
+        out_shape=shape(8, 128),
         in_specs=[SM] * 2 + [VM] * 5 + [HB] * 4 + [VM],
         out_specs=VM,
         scratch_shapes=[
@@ -518,7 +518,7 @@
         grp[None], tf_index, flip, state, curls,
         x_low, x_high, from_left, from_right, in_hbm(from_below_a), in_hbm(from_above_a), tf_table,
     )
-    received = lax.all_to_all(sent, ("grp", "gy"), 0, 0, tiled=True).reshape(groups, depth, 128)
+    received = lax.all_to_all(sent, "gy", 0, 0, tiled=True)
     most = pl.pallas_call(
         depth_kernel,
         out_shape=shape(5, 8, 64, 128),
@@ -527,6 +527,14 @@
         scratch_shapes=[pltpu.VMEM((5, 8, 64, 128), f32)],
         compiler_params=params(6),
     )(after(partly, sent), state, x_low, x_high, from_left, from_right)
+    rays = pl.pallas_call(
+        compose_kernel,
+        out_shape=shape(1, 128),
+        in_specs=[SM, VM, VM],
+        out_specs=VM,
+        compiler_params=params(),
+    )(gy[None], flip, after(received, most))
+    others = [lax.ppermute(rays, "grp", ring("grp", k)) for k in range(1, groups)]
     new_state = pl.pallas_call(
         last_kernel,
         out_shape=shape(5, 8, 64, 128),
@@ -543,12 +551,13 @@
         compiler_params=params(6),
     )(most, in_hbm(from_below_a), from_below_b, in_hbm(from_above_a), from_above_b)
     image = pl.pallas_call(
-        compose_kernel,
+        slot_kernel,
         out_shape=shape(8, 4, 8),
-        in_specs=[SM, SM, SM, VM, VM],
+        in_specs=[SM, SM] + [VM] * 4,
         out_specs=VM,
+        scratch_shapes=[pltpu.VMEM((4, 128), f32)],
         compiler_params=params(),
-    )(grp[None], gy[None], owner[:, 0], flip, after(received, new_state))
+    )(grp[None], owner[:, 0], after(rays, new_state), *others)
     return (new_state, image)
 
 

time: 48.7 us -> 50.4 us (1.035)
  local copies, waits for them, and re-layouts: 1.93 us -> 4.15 us
  waiting for transfers between devices: 5.3 us -> 4.4 us
    ppermute x0 -> x3, starting transfers between devices: none -> 2.89 us  [local(): lax.ppermute(rays, 'grp', ring('grp', k))]
    all_to_all x1, starting transfers between devices: 8.79 us -> 6.46 us  [local(): received = lax.all_to_all(sent, 'gy', 0, 0, tiled=True)]
    unnamed x14 -> x22, local copies, waits for them, and re-layouts: 1.93 us -> 4.15 us
    all_to_all x1, waiting for transfers between devices: 3.05 us -> 1.4 us  [local(): received = lax.all_to_all(sent, 'gy', 0, 0, tiled=True)]
    ppermute x0 -> x3, waiting for transfers between devices: none -> 1.53 us  [local(): lax.ppermute(rays, 'grp', ring('grp', k))]
    pallas_call x1, Pallas kernels: 1.83 us -> 1 us  [local(): pl.pallas_call(depth_kernel, out_shape=shape(5, 8, 64, 128), in_specs=[VM...]
    ppermute x1, waiting for transfers between devices: 2.23 us -> 1.45 us  [local(): from_left = lax.ppermute(x_high, 'gx', ring('gx', 1))]
    pallas_call x1, Pallas kernels: 2.85 us -> 3.49 us  [local(): pl.pallas_call(functools.partial(render_kernel, float(depth * 32)), out_s...]
  transfers between devices with their start and end apart: 9 -> 12, of which waited for: 2 -> 3; matrix products, arithmetic and copies ran while one was open for 0% -> 0% of each run, Pallas kernels for 22% -> 21%
where the time goes in v3:
time: 50.4 us; the launch traced here: 50.1 us
  starting transfers between devices  28.6 us (57%)
  Pallas kernels  12.1 us (24%)
  waiting for transfers between devices  4.4 us (9%)
  local copies, waits for them, and re-layouts  4.15 us (8%)
  between operations  0.78 us (2%)
    ppermute x1, starting transfers between devices, local(): from_right = lax.ppermute(x_low, 'gx', ring('gx', -1))  8.55 us
    all_to_all x1, starting transfers between devices, local(): received = lax.all_to_all(sent, 'gy', 0, 0, tiled=True)  6.46 us
    unnamed x22, local copies, waits for them, and re-layouts  4.15 us
    pallas_call x1, Pallas kernels, local(): pl.pallas_call(functools.partial(render_kernel, float(depth * 32)), out_s...  3.49 us
    ppermute x1, starting transfers between devices, local(): from_above_b = lax.ppermute(low_b, 'grp', ring('grp', -1))  3.26 us
    ppermute x3, starting transfers between devices, local(): lax.ppermute(rays, 'grp', ring('grp', k))  2.89 us
    ppermute x1, starting transfers between devices, local(): from_above_a = lax.ppermute(low_a, 'grp', ring('grp', -1))  2.8 us
    ppermute x1, starting transfers between devices, local(): from_below_a = lax.ppermute(high_a, 'grp', ring('grp', 1))  2.54 us
  transfers between devices with their start and end apart: 12, of which 3 were waited for; matrix products, arithmetic and copies ran while one was open for 0% of the time, Pallas kernels for 21%

profile of v3, /device:TPU:1, one launch (start us, length us, event | category | flops | bytes accessed | tf_op | source)
XLA Modules:
  0.0 50.1 jit_solution(4876365533104565936)
XLA Ops:
  0.6 1.3 %copy-done = f32[5,8,64,128]{3,2,1,0:T(8,128)S(1)} copy-done((f32[5,8,64,128]{3,2,1,0:T(8,128)S(1)}, f32[5,8,64,128]{3,2,1,0:T(8,128)}, u32[]{:S(2)}) %copy-start) | copy-done | bytes 1310744
  2.0 2.5 %collective-permute-start.4 = (f32[2,4,64,128]{3,2,1,0:T(8,128)S(1)}, f32[2,4,64,128]{3,2,1,0:T(8,128)S(1)}, u32[]{:S(2)}, u32[]{:S(2)}) collective-permute-start(f32[2,4,64,128]{3,2,1,0:T(8,128)S(1)} %get-tuple-element.26), channel_id=1, source_target_pairs={{0,64},{64,128},{128,192},{192,0},{1,65},{65,129},{129,193},{193,1... | collective-permute-start | bytes 786440 | tf_op jit(solution)/shard_map/ppermute | solution.py:461
  4.6 2.8 %collective-permute-start.5 = (f32[2,4,64,128]{3,2,1,0:T(8,128)S(1)}, f32[2,4,64,128]{3,2,1,0:T(8,128)}, u32[]{:S(2)}, u32[]{:S(2)}) collective-permute-start(f32[2,4,64,128]{3,2,1,0:T(8,128)S(1)} %get-tuple-element.27), channel_id=1, source_target_pairs={{0,192},{64,0},{128,64},{192,128},{1,193},{65,1},{129,65},{193,129... | collective-permute-start | bytes 786440 | tf_op jit(solution)/shard_map/ppermute | solution.py:462
  7.3 1.8 %collective-permute-start.1 = (f32[5,4,8,128]{3,2,1,0:T(8,128)S(1)}, f32[5,4,8,128]{3,2,1,0:T(8,128)S(1)}, u32[]{:S(2)}, u32[]{:S(2)}) collective-permute-start(f32[5,4,8,128]{3,2,1,0:T(8,128)S(1)} %get-tuple-element.20), channel_id=1, source_target_pairs={{0,7},{1,0},{2,1},{3,2},{4,3},{5,4},{6,5},{7,6},{8,15},{9,8},{10,9... | collective-permute-start | bytes 245768 | tf_op jit(solution)/shard_map/ppermute | solution.py:464
  9.2 0.3 collective-permute-start
  9.4 0.4 shard_map.70
  9.8 8.5 %collective-permute-start.3 = (f32[5,16,128]{2,1,0:T(8,128)S(1)}, f32[5,16,128]{2,1,0:T(8,128)S(1)}, u32[]{:S(2)}, u32[]{:S(2)}) collective-permute-start(f32[5,16,128]{2,1,0:T(8,128)S(1)} %get-tuple-element.24.x_low.refs_0_), channel_id=1, source_target_pairs={{0,56},{8,0},{16,8},{24,16},{32,24},{40,32},{48,40},{56,48},{1,57}... | collective-permute-start | bytes 122888 | tf_op jit(solution)/shard_map/ppermute | solution.py:473
  18.5 0.9 %shard_map.73 = (f32[3,4,64,128]{3,2,1,0:T(8,128)}, f32[3,4,64,128]{3,2,1,0:T(8,128)}) custom-call(f32[5,8,64,128]{3,2,1,0:T(8,128)S(1)} %copy-done), custom_call_target="tpu_custom_call" | custom-call | flops 300000000 | bytes 1000000 | tf_op jit(solution)/shard_map/pallas_call | solution.py:489
  19.4 2.5 %shard_map.69 = (f32[5,8,64,128]{3,2,1,0:T(8,128)S(1)}, f32[3,8,64,128]{3,2,1,0:T(8,128)S(1)}) custom-call(f32[5,8,64,128]{3,2,1,0:T(8,128)S(1)} %copy-done.1, f32[5,4,8,128]{3,2,1,0:T(8,128)S(1)} %collective-permute-done.from_south, f32[5,4,8,128]{3,2,1,0:T(8,128)S(1)} %collective-permute-done.1.from_north), custom_call_target="tpu_custom_call" | custom-call | flops 300000000 | bytes 1000000 | tf_op jit(solution)/shard_map/pallas_call | solution.py:474
  21.9 0.7 %copy-done.10 = f32[2,4,64,128]{3,2,1,0:T(8,128)} copy-done((f32[2,4,64,128]{3,2,1,0:T(8,128)}, f32[2,4,64,128]{3,2,1,0:T(8,128)S(1)}, u32[]{:S(2)}) %copy-start.10) | copy-done | bytes 262168
  22.7 3.3 %collective-permute-start.7 = (f32[3,4,64,128]{3,2,1,0:T(8,128)}, f32[3,4,64,128]{3,2,1,0:T(8,128)S(1)}, u32[]{:S(2)}, u32[]{:S(2)}) collective-permute-start(f32[3,4,64,128]{3,2,1,0:T(8,128)} %get-tuple-element.33), channel_id=1, source_target_pairs={{0,192},{64,0},{128,64},{192,128},{1,193},{65,1},{129,65},{193,129... | collective-permute-start | bytes 1179656 | tf_op jit(solution)/shard_map/ppermute | solution.py:498
  25.9 1.5 %collective-permute-done.2.left_in.refs_2_ = f32[5,16,128]{2,1,0:T(8,128)S(1)} collective-permute-done((f32[5,16,128]{2,1,0:T(8,128)S(1)}, f32[5,16,128]{2,1,0:T(8,128)S(1)}, u32[]{:S(2)}, u32[]{:S(2)}) %collective-permute-start.2) | collective-permute-done | bytes 40992 | tf_op jit(solution)/shard_map/ppermute | solution.py:472
  27.4 3.5 %shard_map.71 = f32[8,128]{1,0:T(8,128)} custom-call(s32[1]{0:T(128)} %bitcast.grp.me, s32[16]{0:T(128)S(1)} %copy-done.9, s32[1,64]{1,0:T(1,128)S(1)} %bitcast.10, f32[5,8,64,128]{3,2,1,0:T(8,128)S(1)} %copy-done.1, f32[3,8,64,128]{3,2,1,0:T(8,128)S(1)} %get-tuple-element.22.curls, f32[5,16,128]{2,1,0:T(8,128)S(1)} %get-tuple-element.24.x_low.refs_0_, ...), custom_call_target="tpu_custom_call" | custom-call | flops 60000002048 | bytes 1000000 | tf_op jit(solution)/shard_map/pallas_call | solution.py:502
  30.9 6.5 %all-to-all-start = ((f32[8,1,128]{2,1,0:T(1,128)}), f32[8,1,128]{2,1,0:T(1,128)S(1)}, u32[]{:S(2)}, u32[]{:S(2)}) async-start(f32[8,1,128]{2,1,0:T(1,128)} %bitcast.5), calls=%async_computation | async-start | bytes 8192 | tf_op jit(solution)/shard_map/all_to_all | solution.py:521
  37.4 1.3 %copy-done.3 = f32[5,8,64,128]{3,2,1,0:T(8,128)S(1)} copy-done((f32[5,8,64,128]{3,2,1,0:T(8,128)S(1)}, f32[5,8,64,128]{3,2,1,0:T(8,128)}, u32[]{:S(2)}) %copy-start.3) | copy-done | bytes 1310744
  38.7 0.8 %copy-done.5 = f32[5,16,128]{2,1,0:T(8,128)S(1)} copy-done((f32[5,16,128]{2,1,0:T(8,128)S(1)}, f32[5,16,128]{2,1,0:T(8,128)}, u32[]{:S(2)}) %copy-start.5) | copy-done | bytes 40984
  39.5 1.0 %shard_map.72.partly = f32[5,8,64,128]{3,2,1,0:T(8,128)S(1)} custom-call(f32[5,8,64,128]{3,2,1,0:T(8,128)S(1)} %copy-done.3, f32[5,8,64,128]{3,2,1,0:T(8,128)S(1)} %copy-done.1, f32[5,16,128]{2,1,0:T(8,128)S(1)} %get-tuple-element.24.x_low.refs_0_, f32[5,16,128]{2,1,0:T(8,128)S(1)} %get-tuple-element.25.x_high.refs_1_, f32[5,16,128]{2,1,0:T(8,128)S(1)} %copy-done.5, ...), custom_call_target="tpu_custom_call" | custom-call | tf_op jit(solution)/shard_map/pallas_call | solution.py:522
  40.5 1.4 %all-to-all-done = f32[8,1,128]{2,1,0:T(1,128)S(1)} async-done(((f32[8,1,128]{2,1,0:T(1,128)}), f32[8,1,128]{2,1,0:T(1,128)S(1)}, u32[]{:S(2)}, u32[]{:S(2)}) %all-to-all-start) | async-done | bytes 4128 | tf_op jit(solution)/shard_map/all_to_all | solution.py:521
  41.9 0.2 shard_map.75.own
  42.0 2.5 %collective-permute-start.10 = (f32[1,128]{1,0:T(1,128)S(1)}, f32[1,128]{1,0:T(1,128)S(1)}, u32[]{:S(2)}, u32[]{:S(2)}) collective-permute-start(f32[1,128]{1,0:T(1,128)S(1)} %shard_map.75.own), channel_id=1, source_target_pairs={{0,192},{64,0},{128,64},{192,128},{1,193},{65,1},{129,65},{193,129... | collective-permute-start | bytes 1544 | tf_op jit(solution)/shard_map/ppermute | solution.py:537
  44.6 0.4 collective-permute-start.9
  44.9 2.3 %shard_map.74 = f32[5,8,64,128]{3,2,1,0:T(8,128)} custom-call(f32[5,8,64,128]{3,2,1,0:T(8,128)S(1)} %shard_map.72.partly, f32[2,4,64,128]{3,2,1,0:T(8,128)} %copy-done.10, f32[3,4,64,128]{3,2,1,0:T(8,128)S(1)} %collective-permute-done.6.refs_1_, f32[2,4,64,128]{3,2,1,0:T(8,128)} %collective-permute-done.5.above_a.refs_2_, ...), custom_call_target="tpu_custom_call" | custom-call | tf_op jit(solution)/shard_map/pallas_call | solution.py:538
  47.2 1.5 %collective-permute-done.8.first = f32[1,128]{1,0:T(1,128)S(1)} collective-permute-done((f32[1,128]{1,0:T(1,128)S(1)}, f32[1,128]{1,0:T(1,128)S(1)}, u32[]{:S(2)}, u32[]{:S(2)}) %collective-permute-start.8) | collective-permute-done | bytes 544 | tf_op jit(solution)/shard_map/ppermute | solution.py:537
  48.8 1.3 %shard_map.76 = f32[8,4,8]{2,1,0:T(4,128)} custom-call(s32[1]{0:T(128)} %bitcast.grp.me, s32[16]{0:T(128)S(1)} %bitcast.9, f32[1,128]{1,0:T(1,128)S(1)} %shard_map.75.own, f32[1,128]{1,0:T(1,128)S(1)} %collective-permute-done.8.first, f32[1,128]{1,0:T(1,128)S(1)} %collective-permute-done.9.second, f32[1,128]{1,0:T(1,128)S(1)} %collective-permute-done.10.third), custom_call_target="tpu_custom_call" | custom-call | tf_op jit(solution)/shard_map/pallas_call | solution.py:553
  (31 shorter events, 0.2 us)
Async XLA Ops:
  0.6 1.3 %copy-start = (f32[5,8,64,128]{3,2,1,0:T(8,128)S(1)}, f32[5,8,64,128]{3,2,1,0:T(8,128)}, u32[]{:S(2)}) copy-start(f32[5,8,64,128]{3,2,1,0:T(8,128)} %state.7) | copy-start | bytes 3932164
  2.0 19.9 %collective-permute-start.4 = (f32[2,4,64,128]{3,2,1,0:T(8,128)S(1)}, f32[2,4,64,128]{3,2,1,0:T(8,128)S(1)}, u32[]{:S(2)}, u32[]{:S(2)}) collective-permute-start(f32[2,4,64,128]{3,2,1,0:T(8,128)S(1)} %get-tuple-element.26), channel_id=1, source_target_pairs={{0,64},{64,128},{128,192},{192,0},{1,65},{65,129},{129,193},{193,1... | collective-permute-start | bytes 786440 | tf_op jit(solution)/shard_map/ppermute | solution.py:461
  4.6 17.4 %collective-permute-start.5 = (f32[2,4,64,128]{3,2,1,0:T(8,128)S(1)}, f32[2,4,64,128]{3,2,1,0:T(8,128)}, u32[]{:S(2)}, u32[]{:S(2)}) collective-permute-start(f32[2,4,64,128]{3,2,1,0:T(8,128)S(1)} %get-tuple-element.27), channel_id=1, source_target_pairs={{0,192},{64,0},{128,64},{192,128},{1,193},{65,1},{129,65},{193,129... | collective-permute-start | bytes 786440 | tf_op jit(solution)/shard_map/ppermute | solution.py:462
  7.3 11.0 %collective-permute-start.1 = (f32[5,4,8,128]{3,2,1,0:T(8,128)S(1)}, f32[5,4,8,128]{3,2,1,0:T(8,128)S(1)}, u32[]{:S(2)}, u32[]{:S(2)}) collective-permute-start(f32[5,4,8,128]{3,2,1,0:T(8,128)S(1)} %get-tuple-element.20), channel_id=1, source_target_pairs={{0,7},{1,0},{2,1},{3,2},{4,3},{5,4},{6,5},{7,6},{8,15},{9,8},{10,9... | collective-permute-start | bytes 245768 | tf_op jit(solution)/shard_map/ppermute | solution.py:464
  9.2 10.3 %copy-start.1 = (f32[5,8,64,128]{3,2,1,0:T(8,128)S(1)}, f32[5,8,64,128]{3,2,1,0:T(8,128)}, u32[]{:S(2)}) copy-start(f32[5,8,64,128]{3,2,1,0:T(8,128)} %state.7) | copy-start | bytes 3932164
  9.2 10.3 %collective-permute-start = (f32[5,4,8,128]{3,2,1,0:T(8,128)S(1)}, f32[5,4,8,128]{3,2,1,0:T(8,128)S(1)}, u32[]{:S(2)}, u32[]{:S(2)}) collective-permute-start(f32[5,4,8,128]{3,2,1,0:T(8,128)S(1)} %get-tuple-element.19), channel_id=1, source_target_pairs={{0,1},{1,2},{2,3},{3,4},{4,5},{5,6},{6,7},{7,0},{8,9},{9,10},{10,1... | collective-permute-start | bytes 245768 | tf_op jit(solution)/shard_map/ppermute | solution.py:463
  9.8 16.1 %collective-permute-start.3 = (f32[5,16,128]{2,1,0:T(8,128)S(1)}, f32[5,16,128]{2,1,0:T(8,128)S(1)}, u32[]{:S(2)}, u32[]{:S(2)}) collective-permute-start(f32[5,16,128]{2,1,0:T(8,128)S(1)} %get-tuple-element.24.x_low.refs_0_), channel_id=1, source_target_pairs={{0,56},{8,0},{16,8},{24,16},{32,24},{40,32},{48,40},{56,48},{1,57}... | collective-permute-start | bytes 122888 | tf_op jit(solution)/shard_map/ppermute | solution.py:473
  18.4 9.0 %copy-start.7 = (s32[64]{0:T(128)S(1)}, s32[64]{0:T(128)}, u32[]{:S(2)}) copy-start(s32[64]{0:T(128)} %param.9) | copy-start | bytes 772
  18.4 9.0 %copy-start.8 = (f32[4,4,256]{2,1,0:T(4,128)S(1)}, f32[4,4,256]{2,1,0:T(4,128)}, u32[]{:S(2)}) copy-start(f32[4,4,256]{2,1,0:T(4,128)} %tables.1) | copy-start | bytes 49156
  18.4 9.0 %copy-start.9 = (s32[16]{0:T(128)S(1)}, s32[16]{0:T(128)}, u32[]{:S(2)}) copy-start(s32[16]{0:T(128)} %index.1) | copy-start | bytes 196
  18.4 9.0 %collective-permute-start.2 = (f32[5,16,128]{2,1,0:T(8,128)S(1)}, f32[5,16,128]{2,1,0:T(8,128)S(1)}, u32[]{:S(2)}, u32[]{:S(2)}) collective-permute-start(f32[5,16,128]{2,1,0:T(8,128)S(1)} %get-tuple-element.25.x_high.refs_1_), channel_id=1, source_target_pairs={{0,8},{8,16},{16,24},{24,32},{32,40},{40,48},{48,56},{56,0},{1,9},... | collective-permute-start | bytes 122888 | tf_op jit(solution)/shard_map/ppermute | solution.py:472
  21.9 9.0 %copy-start.2 = (f32[5,8,64,128]{3,2,1,0:T(8,128)}, f32[5,8,64,128]{3,2,1,0:T(8,128)S(1)}, u32[]{:S(2)}) copy-start(f32[5,8,64,128]{3,2,1,0:T(8,128)S(1)} %get-tuple-element.28.partly) | copy-start | bytes 3932164
  21.9 0.7 %copy-start.10 = (f32[2,4,64,128]{3,2,1,0:T(8,128)}, f32[2,4,64,128]{3,2,1,0:T(8,128)S(1)}, u32[]{:S(2)}) copy-start(f32[2,4,64,128]{3,2,1,0:T(8,128)S(1)} %collective-permute-done.4.below_a.refs_0_) | copy-start | bytes 786436
  22.7 22.3 %collective-permute-start.6 = (f32[3,4,64,128]{3,2,1,0:T(8,128)}, f32[3,4,64,128]{3,2,1,0:T(8,128)S(1)}, u32[]{:S(2)}, u32[]{:S(2)}) collective-permute-start(f32[3,4,64,128]{3,2,1,0:T(8,128)} %get-tuple-element.32), channel_id=1, source_target_pairs={{0,64},{64,128},{128,192},{192,0},{1,65},{65,129},{129,193},{193,1... | collective-permute-start | bytes 1179656 | tf_op jit(solution)/shard_map/ppermute | solution.py:499
  22.7 22.3 %collective-permute-start.7 = (f32[3,4,64,128]{3,2,1,0:T(8,128)}, f32[3,4,64,128]{3,2,1,0:T(8,128)S(1)}, u32[]{:S(2)}, u32[]{:S(2)}) collective-permute-start(f32[3,4,64,128]{3,2,1,0:T(8,128)} %get-tuple-element.33), channel_id=1, source_target_pairs={{0,192},{64,0},{128,64},{192,128},{1,193},{65,1},{129,65},{193,129... | collective-permute-start | bytes 1179656 | tf_op jit(solution)/shard_map/ppermute | solution.py:498
  27.4 3.5 %copy-start.4 = (f32[5,16,128]{2,1,0:T(8,128)}, f32[5,16,128]{2,1,0:T(8,128)S(1)}, u32[]{:S(2)}) copy-start(f32[5,16,128]{2,1,0:T(8,128)S(1)} %collective-permute-done.2.left_in.refs_2_) | copy-start | bytes 122884
  30.9 11.0 %all-to-all-start = ((f32[8,1,128]{2,1,0:T(1,128)}), f32[8,1,128]{2,1,0:T(1,128)S(1)}, u32[]{:S(2)}, u32[]{:S(2)}) async-start(f32[8,1,128]{2,1,0:T(1,128)} %bitcast.5), calls=%async_computation | async-start | bytes 8192 | tf_op jit(solution)/shard_map/all_to_all | solution.py:521
  37.4 1.3 %copy-start.3 = (f32[5,8,64,128]{3,2,1,0:T(8,128)S(1)}, f32[5,8,64,128]{3,2,1,0:T(8,128)}, u32[]{:S(2)}) copy-start(f32[5,8,64,128]{3,2,1,0:T(8,128)} %copy-done.2) | copy-start | bytes 3932164
  38.7 0.8 %copy-start.5 = (f32[5,16,128]{2,1,0:T(8,128)S(1)}, f32[5,16,128]{2,1,0:T(8,128)}, u32[]{:S(2)}) copy-start(f32[5,16,128]{2,1,0:T(8,128)} %copy-done.4) | copy-start | bytes 122884
  42.0 6.7 %copy-start.6 = (s32[16,1]{0,1:T(1,128)S(1)}, s32[16,1]{0,1:T(1,128)}, u32[]{:S(2)}) copy-start(s32[16,1]{0,1:T(1,128)} %param.7) | copy-start | bytes 196
  42.0 5.2 %collective-permute-start.10 = (f32[1,128]{1,0:T(1,128)S(1)}, f32[1,128]{1,0:T(1,128)S(1)}, u32[]{:S(2)}, u32[]{:S(2)}) collective-permute-start(f32[1,128]{1,0:T(1,128)S(1)} %shard_map.75.own), channel_id=1, source_target_pairs={{0,192},{64,0},{128,64},{192,128},{1,193},{65,1},{129,65},{193,129... | collective-permute-start | bytes 1544 | tf_op jit(solution)/shard_map/ppermute | solution.py:537
  44.6 4.2 %collective-permute-start.8 = (f32[1,128]{1,0:T(1,128)S(1)}, f32[1,128]{1,0:T(1,128)S(1)}, u32[]{:S(2)}, u32[]{:S(2)}) collective-permute-start(f32[1,128]{1,0:T(1,128)S(1)} %shard_map.75.own), channel_id=1, source_target_pairs={{0,64},{64,128},{128,192},{192,0},{1,65},{65,129},{129,193},{193,1... | collective-permute-start | bytes 1544 | tf_op jit(solution)/shard_map/ppermute | solution.py:537
  44.6 4.2 %collective-permute-start.9 = (f32[1,128]{1,0:T(1,128)S(1)}, f32[1,128]{1,0:T(1,128)S(1)}, u32[]{:S(2)}, u32[]{:S(2)}) collective-permute-start(f32[1,128]{1,0:T(1,128)S(1)} %shard_map.75.own), channel_id=1, source_target_pairs={{0,128},{64,192},{128,0},{192,64},{1,129},{65,193},{129,1},{193,65... | collective-permute-start | bytes 1544 | tf_op jit(solution)/shard_map/ppermute | solution.py:537

commit v4 on v2

--- a/solution.py
+++ b/solution.py
@@ -56,12 +56,24 @@
     return mz, mz * u, mz * v, mz * w + p, (energy + p) * w
 
 
-def first_pack_kernel(state, low, high, y_low, y_high):
-    for z in range(8):
-        inverse = 1.0 / state[0, z]
-        into = low if z < 4 else high
-        into[0, z % 4] = state[1, z] * inverse
-        into[1, z % 4] = state[2, z] * inverse
+def first_pack_kernel(state, low, high, held, sems):
+    copies = [
+        pltpu.make_async_copy(state.at[c, pl.ds(4 * h, 4)], held.at[c, pl.ds(4 * h, 4)], sems.at[3 * h + c])
+        for h in range(2)
+        for c in range(3)
+    ]
+    for copy in copies:
+        copy.start()
+    for h, into in enumerate((low, high)):
+        for copy in copies[3 * h : 3 * h + 3]:
+            copy.wait()
+        for z in range(4):
+            inverse = 1.0 / held[0, 4 * h + z]
+            into[0, z] = held[1, 4 * h + z] * inverse
+            into[1, z] = held[2, 4 * h + z] * inverse
+
+
+def row_pack_kernel(state, y_low, y_high):
     sub = lax.broadcasted_iota(jnp.int32, (8, 128), 0)
     for c in range(5):
         for k in range(4):
@@ -451,13 +463,21 @@
     grp = lax.axis_index("grp")
     gy = lax.axis_index("gy")
     groups, depth = lax.axis_size("grp"), lax.axis_size("gy")
-    low_a, high_a, y_low, y_high = pl.pallas_call(
+    low_a, high_a = pl.pallas_call(
         first_pack_kernel,
-        out_shape=(shape(2, 4, 64, 128), shape(2, 4, 64, 128), shape(5, 4, 8, 128), shape(5, 4, 8, 128)),
+        out_shape=(shape(2, 4, 64, 128), shape(2, 4, 64, 128)),
+        in_specs=[HB],
+        out_specs=(VM, VM),
+        scratch_shapes=[pltpu.VMEM((3, 8, 64, 128), f32), pltpu.SemaphoreType.DMA((6,))],
+        compiler_params=params(),
+    )(in_hbm(state))
+    y_low, y_high = pl.pallas_call(
+        row_pack_kernel,
+        out_shape=(shape(5, 4, 8, 128), shape(5, 4, 8, 128)),
         in_specs=[VM],
-        out_specs=(VM, VM, VM, VM),
+        out_specs=(VM, VM),
         compiler_params=params(),
-    )(state)
+    )(after(state, low_a))
     from_below_a = lax.ppermute(high_a, "grp", ring("grp", 1))
     from_above_a = lax.ppermute(low_a, "grp", ring("grp", -1))
     from_south = lax.ppermute(y_high, "gy", ring("gy", 1))

time: 48.7 us -> 47.6 us (0.977)
  starting transfers between devices: 28.2 us -> 24.4 us
  waiting for transfers between devices: 5.3 us -> 7.96 us
  local copies, waits for them, and re-layouts: 1.93 us -> 0.62 us
  Pallas kernels: 12.3 us -> 13.6 us
    ppermute x1, starting transfers between devices: 2.54 us -> 0.01 us  [local(): from_below_a = lax.ppermute(high_a, 'grp', ring('grp', 1))]
    ppermute x1, starting transfers between devices: 2.8 us -> 5.25 us  [local(): from_above_a = lax.ppermute(low_a, 'grp', ring('grp', -1))]
    all_to_all x1, starting transfers between devices: 8.79 us -> 6.55 us  [local(): lax.all_to_all(sent, ('grp', 'gy'), 0, 0, tiled=True)]
    ppermute x1, starting transfers between devices: 8.55 us -> 6.84 us  [local(): from_right = lax.ppermute(x_low, 'gx', ring('gx', -1))]
    ppermute x1, waiting for transfers between devices: 2.23 us -> 3.9 us  [local(): from_left = lax.ppermute(x_high, 'gx', ring('gx', 1))]
    pallas_call x1, Pallas kernels: 0.06 us -> 1.37 us  [local(): pl.pallas_call(first_pack_kernel, out_shape=(shape(2, 4, 64, 128), shape(...]
    unnamed x14 -> x12, local copies, waits for them, and re-layouts: 1.93 us -> 0.62 us
    ppermute x1, waiting for transfers between devices: 0.01 us -> 0.99 us  [local(): from_right = lax.ppermute(x_low, 'gx', ring('gx', -1))]
  transfers between devices with their start and end apart: 9 -> 9, of which waited for: 2 -> 3; matrix products, arithmetic and copies ran while one was open for 0% -> 0% of each run, Pallas kernels for 22% -> 23%
where the time goes in v4:
time: 47.6 us; the launch traced here: 47.4 us
  starting transfers between devices  24.4 us (51%)
  Pallas kernels  13.6 us (29%)
  waiting for transfers between devices  7.96 us (17%)
  between operations  0.76 us (2%)
  local copies, waits for them, and re-layouts  0.62 us (1%)
    ppermute x1, starting transfers between devices, local(): from_right = lax.ppermute(x_low, 'gx', ring('gx', -1))  6.84 us
    all_to_all x1, starting transfers between devices, local(): lax.all_to_all(sent, ('grp', 'gy'), 0, 0, tiled=True)  6.55 us
    ppermute x1, starting transfers between devices, local(): from_above_a = lax.ppermute(low_a, 'grp', ring('grp', -1))  5.25 us
    ppermute x1, waiting for transfers between devices, local(): from_left = lax.ppermute(x_high, 'gx', ring('gx', 1))  3.9 us
    all_to_all x1, waiting for transfers between devices, local(): lax.all_to_all(sent, ('grp', 'gy'), 0, 0, tiled=True)  3.05 us
    pallas_call x1, Pallas kernels, local(): pl.pallas_call(functools.partial(render_kernel, float(depth * 32)), out_s...  2.85 us
    ppermute x1, starting transfers between devices, local(): from_above_b = lax.ppermute(low_b, 'grp', ring('grp', -1))  2.8 us
    pallas_call x1, Pallas kernels, local(): pl.pallas_call(inner_kernel, out_shape=(shape(5, 8, 64, 128), shape(3, 8,...  2.45 us
  transfers between devices with their start and end apart: 9, of which 3 were waited for; matrix products, arithmetic and copies ran while one was open for 0% of the time, Pallas kernels for 23%

profile of v4, /device:TPU:1, one launch (start us, length us, event | category | flops | bytes accessed | tf_op | source)
XLA Modules:
  0.0 47.4 jit_solution(5914795535555383784)
XLA Ops:
  0.6 1.4 %shard_map.68 = (f32[2,4,64,128]{3,2,1,0:T(8,128)S(1)}, f32[2,4,64,128]{3,2,1,0:T(8,128)S(1)}) custom-call(f32[5,8,64,128]{3,2,1,0:T(8,128)} %state.8), custom_call_target="tpu_custom_call" | custom-call | tf_op jit(solution)/shard_map/pallas_call | solution.py:466
  2.0 5.3 %collective-permute-start.5 = (f32[2,4,64,128]{3,2,1,0:T(8,128)S(1)}, f32[2,4,64,128]{3,2,1,0:T(8,128)}, u32[]{:S(2)}, u32[]{:S(2)}) collective-permute-start(f32[2,4,64,128]{3,2,1,0:T(8,128)S(1)} %get-tuple-element.19), channel_id=1, source_target_pairs={{0,192},{64,0},{128,64},{192,128},{1,193},{65,1},{129,65},{193,129... | collective-permute-start | bytes 786440 | tf_op jit(solution)/shard_map/ppermute | solution.py:482
  7.3 0.0 collective-permute-start.4
  7.3 1.0 %collective-permute-start.1 = (f32[5,4,8,128]{3,2,1,0:T(8,128)S(1)}, f32[5,4,8,128]{3,2,1,0:T(8,128)S(1)}, u32[]{:S(2)}, u32[]{:S(2)}) collective-permute-start(f32[5,4,8,128]{3,2,1,0:T(8,128)S(1)} %get-tuple-element.22), channel_id=1, source_target_pairs={{0,7},{1,0},{2,1},{3,2},{4,3},{5,4},{6,5},{7,6},{8,15},{9,8},{10,9... | collective-permute-start | bytes 245768 | tf_op jit(solution)/shard_map/ppermute | solution.py:484
  8.3 1.1 %collective-permute-start = (f32[5,4,8,128]{3,2,1,0:T(8,128)S(1)}, f32[5,4,8,128]{3,2,1,0:T(8,128)S(1)}, u32[]{:S(2)}, u32[]{:S(2)}) collective-permute-start(f32[5,4,8,128]{3,2,1,0:T(8,128)S(1)} %get-tuple-element.21), channel_id=1, source_target_pairs={{0,1},{1,2},{2,3},{3,4},{4,5},{5,6},{6,7},{7,0},{8,9},{9,10},{10,1... | collective-permute-start | bytes 245768 | tf_op jit(solution)/shard_map/ppermute | solution.py:483
  9.4 0.4 shard_map.71
  9.8 6.8 %collective-permute-start.3 = (f32[5,16,128]{2,1,0:T(8,128)S(1)}, f32[5,16,128]{2,1,0:T(8,128)S(1)}, u32[]{:S(2)}, u32[]{:S(2)}) collective-permute-start(f32[5,16,128]{2,1,0:T(8,128)S(1)} %get-tuple-element.26.x_low.refs_0_), channel_id=1, source_target_pairs={{0,56},{8,0},{16,8},{24,16},{32,24},{40,32},{48,40},{56,48},{1,57}... | collective-permute-start | bytes 122888 | tf_op jit(solution)/shard_map/ppermute | solution.py:493
  16.7 0.1 collective-permute-start.2
  16.8 0.9 %shard_map.74 = (f32[3,4,64,128]{3,2,1,0:T(8,128)}, f32[3,4,64,128]{3,2,1,0:T(8,128)}) custom-call(f32[5,8,64,128]{3,2,1,0:T(8,128)S(1)} %copy-done), custom_call_target="tpu_custom_call" | custom-call | flops 300000000 | bytes 1000000 | tf_op jit(solution)/shard_map/pallas_call | solution.py:509
  17.7 2.5 %shard_map.70 = (f32[5,8,64,128]{3,2,1,0:T(8,128)S(1)}, f32[3,8,64,128]{3,2,1,0:T(8,128)S(1)}) custom-call(f32[5,8,64,128]{3,2,1,0:T(8,128)S(1)} %copy-done, f32[5,4,8,128]{3,2,1,0:T(8,128)S(1)} %collective-permute-done.from_south, f32[5,4,8,128]{3,2,1,0:T(8,128)S(1)} %collective-permute-done.1.from_north), custom_call_target="tpu_custom_call" | custom-call | flops 300000000 | bytes 1000000 | tf_op jit(solution)/shard_map/pallas_call | solution.py:494
  20.2 0.0 collective-permute-done.4.below_a.refs_0_
  20.2 0.8 %collective-permute-start.6 = (f32[3,4,64,128]{3,2,1,0:T(8,128)}, f32[3,4,64,128]{3,2,1,0:T(8,128)S(1)}, u32[]{:S(2)}, u32[]{:S(2)}) collective-permute-start(f32[3,4,64,128]{3,2,1,0:T(8,128)} %get-tuple-element.33), channel_id=1, source_target_pairs={{0,64},{64,128},{128,192},{192,0},{1,65},{65,129},{129,193},{193,1... | collective-permute-start | bytes 1179656 | tf_op jit(solution)/shard_map/ppermute | solution.py:519
  21.0 2.8 %collective-permute-start.7 = (f32[3,4,64,128]{3,2,1,0:T(8,128)}, f32[3,4,64,128]{3,2,1,0:T(8,128)S(1)}, u32[]{:S(2)}, u32[]{:S(2)}) collective-permute-start(f32[3,4,64,128]{3,2,1,0:T(8,128)} %get-tuple-element.34), channel_id=1, source_target_pairs={{0,192},{64,0},{128,64},{192,128},{1,193},{65,1},{129,65},{193,129... | collective-permute-start | bytes 1179656 | tf_op jit(solution)/shard_map/ppermute | solution.py:518
  23.8 1.0 %collective-permute-done.3.right_in.refs_3_ = f32[5,16,128]{2,1,0:T(8,128)S(1)} collective-permute-done((f32[5,16,128]{2,1,0:T(8,128)S(1)}, f32[5,16,128]{2,1,0:T(8,128)S(1)}, u32[]{:S(2)}, u32[]{:S(2)}) %collective-permute-start.3) | collective-permute-done | bytes 40992 | tf_op jit(solution)/shard_map/ppermute | solution.py:493
  24.8 3.9 %collective-permute-done.2.left_in.refs_2_ = f32[5,16,128]{2,1,0:T(8,128)} collective-permute-done((f32[5,16,128]{2,1,0:T(8,128)S(1)}, f32[5,16,128]{2,1,0:T(8,128)}, u32[]{:S(2)}, u32[]{:S(2)}) %collective-permute-start.2) | collective-permute-done | bytes 40992 | tf_op jit(solution)/shard_map/ppermute | solution.py:492
  28.7 2.8 %shard_map.72 = f32[32,128]{1,0:T(8,128)S(1)} custom-call(s32[1]{0:T(128)} %bitcast.grp.me, s32[16]{0:T(128)S(1)} %copy-done.5, s32[1,64]{1,0:T(1,128)S(1)} %bitcast.11, f32[5,8,64,128]{3,2,1,0:T(8,128)S(1)} %copy-done, f32[3,8,64,128]{3,2,1,0:T(8,128)S(1)} %get-tuple-element.24.curls, f32[5,16,128]{2,1,0:T(8,128)S(1)} %get-tuple-element.26.x_low.refs_0_, ...), custom_call_target="tpu_custom_call" | custom-call | flops 60000002048 | bytes 1000000 | tf_op jit(solution)/shard_map/pallas_call | solution.py:522
  31.5 0.0 copy-start.1
  31.5 0.6 %copy-done.1 = f32[32,128]{1,0:T(8,128)} copy-done((f32[32,128]{1,0:T(8,128)}, f32[32,128]{1,0:T(8,128)S(1)}, u32[]{:S(2)}) %copy-start.1) | copy-done | bytes 16408
  32.1 6.6 %all-to-all-start = ((f32[32,1,128]{2,1,0:T(1,128)}), f32[32,1,128]{2,1,0:T(1,128)S(1)}, u32[]{:S(2)}, u32[]{:S(2)}) async-start(f32[32,1,128]{2,1,0:T(1,128)} %bitcast.9), calls=%async_computation | async-start | bytes 32768 | tf_op jit(solution)/shard_map/all_to_all | solution.py:541
  38.7 1.8 %shard_map.73.partly = f32[5,8,64,128]{3,2,1,0:T(8,128)S(1)} custom-call(f32[5,8,64,128]{3,2,1,0:T(8,128)S(1)} %get-tuple-element.29.partly, f32[5,8,64,128]{3,2,1,0:T(8,128)S(1)} %copy-done, f32[5,16,128]{2,1,0:T(8,128)S(1)} %get-tuple-element.26.x_low.refs_0_, f32[5,16,128]{2,1,0:T(8,128)S(1)} %get-tuple-element.27.x_high.refs_1_, ...), custom_call_target="tpu_custom_call" | custom-call | tf_op jit(solution)/shard_map/pallas_call | solution.py:542
  40.5 0.0 copy-start.2
  40.6 2.3 %shard_map.75 = f32[5,8,64,128]{3,2,1,0:T(8,128)} custom-call(f32[5,8,64,128]{3,2,1,0:T(8,128)S(1)} %shard_map.73.partly, f32[2,4,64,128]{3,2,1,0:T(8,128)} %collective-permute-done.4.below_a.refs_0_, f32[3,4,64,128]{3,2,1,0:T(8,128)S(1)} %collective-permute-done.6.refs_1_, f32[2,4,64,128]{3,2,1,0:T(8,128)} %collective-permute-done.5.above_a.refs_2_, ...), custom_call_target="tpu_custom_call" | custom-call | tf_op jit(solution)/shard_map/pallas_call | solution.py:550
  42.9 3.0 %all-to-all-done = f32[32,1,128]{2,1,0:T(1,128)S(1)} async-done(((f32[32,1,128]{2,1,0:T(1,128)}), f32[32,1,128]{2,1,0:T(1,128)S(1)}, u32[]{:S(2)}, u32[]{:S(2)}) %all-to-all-start) | async-done | bytes 16416 | tf_op jit(solution)/shard_map/all_to_all | solution.py:541
  45.9 1.5 %shard_map.76 = f32[8,4,8]{2,1,0:T(4,128)} custom-call(s32[1]{0:T(128)} %bitcast.grp.me, s32[1]{0:T(128)} %bitcast.2.depth, s32[16]{0:T(128)S(1)} %bitcast.10, s32[1,64]{1,0:T(1,128)S(1)} %bitcast.12, f32[4,8,128]{2,1,0:T(8,128)S(1)} %bitcast.8), custom_call_target="tpu_custom_call" | custom-call | tf_op jit(solution)/shard_map/pallas_call | solution.py:565
  (15 shorter events, 0.1 us)
Async XLA Ops:
  0.6 6.6 %copy-start = (f32[5,8,64,128]{3,2,1,0:T(8,128)S(1)}, f32[5,8,64,128]{3,2,1,0:T(8,128)}, u32[]{:S(2)}) copy-start(f32[5,8,64,128]{3,2,1,0:T(8,128)} %state.8) | copy-start | bytes 3932164
  2.0 18.1 %collective-permute-start.5 = (f32[2,4,64,128]{3,2,1,0:T(8,128)S(1)}, f32[2,4,64,128]{3,2,1,0:T(8,128)}, u32[]{:S(2)}, u32[]{:S(2)}) collective-permute-start(f32[2,4,64,128]{3,2,1,0:T(8,128)S(1)} %get-tuple-element.19), channel_id=1, source_target_pairs={{0,192},{64,0},{128,64},{192,128},{1,193},{65,1},{129,65},{193,129... | collective-permute-start | bytes 786440 | tf_op jit(solution)/shard_map/ppermute | solution.py:482
  7.3 12.9 %collective-permute-start.4 = (f32[2,4,64,128]{3,2,1,0:T(8,128)S(1)}, f32[2,4,64,128]{3,2,1,0:T(8,128)}, u32[]{:S(2)}, u32[]{:S(2)}) collective-permute-start(f32[2,4,64,128]{3,2,1,0:T(8,128)S(1)} %get-tuple-element.28), channel_id=1, source_target_pairs={{0,64},{64,128},{128,192},{192,0},{1,65},{65,129},{129,193},{193,1... | collective-permute-start | bytes 786440 | tf_op jit(solution)/shard_map/ppermute | solution.py:481
  7.3 9.3 %collective-permute-start.1 = (f32[5,4,8,128]{3,2,1,0:T(8,128)S(1)}, f32[5,4,8,128]{3,2,1,0:T(8,128)S(1)}, u32[]{:S(2)}, u32[]{:S(2)}) collective-permute-start(f32[5,4,8,128]{3,2,1,0:T(8,128)S(1)} %get-tuple-element.22), channel_id=1, source_target_pairs={{0,7},{1,0},{2,1},{3,2},{4,3},{5,4},{6,5},{7,6},{8,15},{9,8},{10,9... | collective-permute-start | bytes 245768 | tf_op jit(solution)/shard_map/ppermute | solution.py:484
  8.3 9.4 %collective-permute-start = (f32[5,4,8,128]{3,2,1,0:T(8,128)S(1)}, f32[5,4,8,128]{3,2,1,0:T(8,128)S(1)}, u32[]{:S(2)}, u32[]{:S(2)}) collective-permute-start(f32[5,4,8,128]{3,2,1,0:T(8,128)S(1)} %get-tuple-element.21), channel_id=1, source_target_pairs={{0,1},{1,2},{2,3},{3,4},{4,5},{5,6},{6,7},{7,0},{8,9},{9,10},{10,1... | collective-permute-start | bytes 245768 | tf_op jit(solution)/shard_map/ppermute | solution.py:483
  9.8 15.0 %collective-permute-start.3 = (f32[5,16,128]{2,1,0:T(8,128)S(1)}, f32[5,16,128]{2,1,0:T(8,128)S(1)}, u32[]{:S(2)}, u32[]{:S(2)}) collective-permute-start(f32[5,16,128]{2,1,0:T(8,128)S(1)} %get-tuple-element.26.x_low.refs_0_), channel_id=1, source_target_pairs={{0,56},{8,0},{16,8},{24,16},{32,24},{40,32},{48,40},{56,48},{1,57}... | collective-permute-start | bytes 122888 | tf_op jit(solution)/shard_map/ppermute | solution.py:493
  16.6 12.0 %copy-start.3 = (s32[64]{0:T(128)S(1)}, s32[64]{0:T(128)}, u32[]{:S(2)}) copy-start(s32[64]{0:T(128)} %param.9) | copy-start | bytes 772
  16.6 12.0 %copy-start.4 = (f32[4,4,256]{2,1,0:T(4,128)S(1)}, f32[4,4,256]{2,1,0:T(4,128)}, u32[]{:S(2)}) copy-start(f32[4,4,256]{2,1,0:T(4,128)} %tables.1) | copy-start | bytes 49156
  16.6 12.0 %copy-start.5 = (s32[16]{0:T(128)S(1)}, s32[16]{0:T(128)}, u32[]{:S(2)}) copy-start(s32[16]{0:T(128)} %index.1) | copy-start | bytes 196
  16.7 12.0 %collective-permute-start.2 = (f32[5,16,128]{2,1,0:T(8,128)S(1)}, f32[5,16,128]{2,1,0:T(8,128)}, u32[]{:S(2)}, u32[]{:S(2)}) collective-permute-start(f32[5,16,128]{2,1,0:T(8,128)S(1)} %get-tuple-element.27.x_high.refs_1_), channel_id=1, source_target_pairs={{0,8},{8,16},{16,24},{24,32},{32,40},{40,48},{48,56},{56,0},{1,9},... | collective-permute-start | bytes 122888 | tf_op jit(solution)/shard_map/ppermute | solution.py:492
  20.2 20.4 %collective-permute-start.6 = (f32[3,4,64,128]{3,2,1,0:T(8,128)}, f32[3,4,64,128]{3,2,1,0:T(8,128)S(1)}, u32[]{:S(2)}, u32[]{:S(2)}) collective-permute-start(f32[3,4,64,128]{3,2,1,0:T(8,128)} %get-tuple-element.33), channel_id=1, source_target_pairs={{0,64},{64,128},{128,192},{192,0},{1,65},{65,129},{129,193},{193,1... | collective-permute-start | bytes 1179656 | tf_op jit(solution)/shard_map/ppermute | solution.py:519
  21.0 19.6 %collective-permute-start.7 = (f32[3,4,64,128]{3,2,1,0:T(8,128)}, f32[3,4,64,128]{3,2,1,0:T(8,128)S(1)}, u32[]{:S(2)}, u32[]{:S(2)}) collective-permute-start(f32[3,4,64,128]{3,2,1,0:T(8,128)} %get-tuple-element.34), channel_id=1, source_target_pairs={{0,192},{64,0},{128,64},{192,128},{1,193},{65,1},{129,65},{193,129... | collective-permute-start | bytes 1179656 | tf_op jit(solution)/shard_map/ppermute | solution.py:518
  31.5 0.6 %copy-start.1 = (f32[32,128]{1,0:T(8,128)}, f32[32,128]{1,0:T(8,128)S(1)}, u32[]{:S(2)}) copy-start(f32[32,128]{1,0:T(8,128)S(1)} %shard_map.72) | copy-start | bytes 49156
  32.1 13.8 %all-to-all-start = ((f32[32,1,128]{2,1,0:T(1,128)}), f32[32,1,128]{2,1,0:T(1,128)S(1)}, u32[]{:S(2)}, u32[]{:S(2)}) async-start(f32[32,1,128]{2,1,0:T(1,128)} %bitcast.9), calls=%async_computation | async-start | bytes 32768 | tf_op jit(solution)/shard_map/all_to_all | solution.py:541
  40.5 5.4 %copy-start.2 = (s32[16,1]{0,1:T(1,128)S(1)}, s32[16,1]{0,1:T(1,128)}, u32[]{:S(2)}) copy-start(s32[16,1]{0,1:T(1,128)} %param.7) | copy-start | bytes 196

commit v5 on v4

--- a/solution.py
+++ b/solution.py
@@ -374,13 +374,12 @@
     ]
     for copy in copies:
         copy.start()
-    for copy in copies:
-        copy.wait()
 
     def sending(c):
         return pltpu.make_async_copy(held.at[c], out.at[c], out_sems.at[c])
 
     for side, (a, b) in enumerate(((below_a, below_b), (above_a, above_b))):
+        copies[side].wait()
         for p in range(4):
             for r in range(0, 64, 16):
                 rows = slice(r, r + 16)

time: 47.6 us -> 47.6 us (level)
  no operation moved by 1% of the time
where the time goes in v5:
time: 47.6 us; the launch traced here: 47.4 us
  starting transfers between devices  24.4 us (51%)
  Pallas kernels  13.6 us (29%)
  waiting for transfers between devices  8.03 us (17%)
  between operations  0.76 us (2%)
  local copies, waits for them, and re-layouts  0.62 us (1%)
    ppermute x1, starting transfers between devices, local(): from_right = lax.ppermute(x_low, 'gx', ring('gx', -1))  6.84 us
    all_to_all x1, starting transfers between devices, local(): lax.all_to_all(sent, ('grp', 'gy'), 0, 0, tiled=True)  6.55 us
    ppermute x1, starting transfers between devices, local(): from_above_a = lax.ppermute(low_a, 'grp', ring('grp', -1))  5.25 us
    ppermute x1, waiting for transfers between devices, local(): from_left = lax.ppermute(x_high, 'gx', ring('gx', 1))  3.9 us
    all_to_all x1, waiting for transfers between devices, local(): lax.all_to_all(sent, ('grp', 'gy'), 0, 0, tiled=True)  3.12 us
    pallas_call x1, Pallas kernels, local(): pl.pallas_call(functools.partial(render_kernel, float(depth * 32)), out_s...  2.85 us
    ppermute x1, starting transfers between devices, local(): from_above_b = lax.ppermute(low_b, 'grp', ring('grp', -1))  2.8 us
    pallas_call x1, Pallas kernels, local(): pl.pallas_call(inner_kernel, out_shape=(shape(5, 8, 64, 128), shape(3, 8,...  2.45 us
  transfers between devices with their start and end apart: 9, of which 3 were waited for; matrix products, arithmetic and copies ran while one was open for 0% of the time, Pallas kernels for 23%

profile of v5, /device:TPU:1, one launch (start us, length us, event | category | flops | bytes accessed | tf_op | source)
XLA Modules:
  0.0 47.4 jit_solution(15461367689706533564)
XLA Ops:
  0.6 1.4 %shard_map.68 = (f32[2,4,64,128]{3,2,1,0:T(8,128)S(1)}, f32[2,4,64,128]{3,2,1,0:T(8,128)S(1)}) custom-call(f32[5,8,64,128]{3,2,1,0:T(8,128)} %state.8), custom_call_target="tpu_custom_call" | custom-call | tf_op jit(solution)/shard_map/pallas_call | solution.py:465
  2.0 5.3 %collective-permute-start.5 = (f32[2,4,64,128]{3,2,1,0:T(8,128)S(1)}, f32[2,4,64,128]{3,2,1,0:T(8,128)}, u32[]{:S(2)}, u32[]{:S(2)}) collective-permute-start(f32[2,4,64,128]{3,2,1,0:T(8,128)S(1)} %get-tuple-element.19), channel_id=1, source_target_pairs={{0,192},{64,0},{128,64},{192,128},{1,193},{65,1},{129,65},{193,129... | collective-permute-start | bytes 786440 | tf_op jit(solution)/shard_map/ppermute | solution.py:481
  7.3 0.0 collective-permute-start.4
  7.3 1.0 %collective-permute-start.1 = (f32[5,4,8,128]{3,2,1,0:T(8,128)S(1)}, f32[5,4,8,128]{3,2,1,0:T(8,128)S(1)}, u32[]{:S(2)}, u32[]{:S(2)}) collective-permute-start(f32[5,4,8,128]{3,2,1,0:T(8,128)S(1)} %get-tuple-element.22), channel_id=1, source_target_pairs={{0,7},{1,0},{2,1},{3,2},{4,3},{5,4},{6,5},{7,6},{8,15},{9,8},{10,9... | collective-permute-start | bytes 245768 | tf_op jit(solution)/shard_map/ppermute | solution.py:483
  8.3 1.1 %collective-permute-start = (f32[5,4,8,128]{3,2,1,0:T(8,128)S(1)}, f32[5,4,8,128]{3,2,1,0:T(8,128)S(1)}, u32[]{:S(2)}, u32[]{:S(2)}) collective-permute-start(f32[5,4,8,128]{3,2,1,0:T(8,128)S(1)} %get-tuple-element.21), channel_id=1, source_target_pairs={{0,1},{1,2},{2,3},{3,4},{4,5},{5,6},{6,7},{7,0},{8,9},{9,10},{10,1... | collective-permute-start | bytes 245768 | tf_op jit(solution)/shard_map/ppermute | solution.py:482
  9.4 0.4 shard_map.71
  9.8 6.8 %collective-permute-start.3 = (f32[5,16,128]{2,1,0:T(8,128)S(1)}, f32[5,16,128]{2,1,0:T(8,128)S(1)}, u32[]{:S(2)}, u32[]{:S(2)}) collective-permute-start(f32[5,16,128]{2,1,0:T(8,128)S(1)} %get-tuple-element.26.x_low.refs_0_), channel_id=1, source_target_pairs={{0,56},{8,0},{16,8},{24,16},{32,24},{40,32},{48,40},{56,48},{1,57}... | collective-permute-start | bytes 122888 | tf_op jit(solution)/shard_map/ppermute | solution.py:492
  16.7 0.1 collective-permute-start.2
  16.8 0.9 %shard_map.74 = (f32[3,4,64,128]{3,2,1,0:T(8,128)}, f32[3,4,64,128]{3,2,1,0:T(8,128)}) custom-call(f32[5,8,64,128]{3,2,1,0:T(8,128)S(1)} %copy-done), custom_call_target="tpu_custom_call" | custom-call | flops 300000000 | bytes 1000000 | tf_op jit(solution)/shard_map/pallas_call | solution.py:508
  17.7 2.5 %shard_map.70 = (f32[5,8,64,128]{3,2,1,0:T(8,128)S(1)}, f32[3,8,64,128]{3,2,1,0:T(8,128)S(1)}) custom-call(f32[5,8,64,128]{3,2,1,0:T(8,128)S(1)} %copy-done, f32[5,4,8,128]{3,2,1,0:T(8,128)S(1)} %collective-permute-done.from_south, f32[5,4,8,128]{3,2,1,0:T(8,128)S(1)} %collective-permute-done.1.from_north), custom_call_target="tpu_custom_call" | custom-call | flops 300000000 | bytes 1000000 | tf_op jit(solution)/shard_map/pallas_call | solution.py:493
  20.2 0.0 collective-permute-done.4.below_a.refs_0_
  20.2 0.8 %collective-permute-start.6 = (f32[3,4,64,128]{3,2,1,0:T(8,128)}, f32[3,4,64,128]{3,2,1,0:T(8,128)S(1)}, u32[]{:S(2)}, u32[]{:S(2)}) collective-permute-start(f32[3,4,64,128]{3,2,1,0:T(8,128)} %get-tuple-element.33), channel_id=1, source_target_pairs={{0,64},{64,128},{128,192},{192,0},{1,65},{65,129},{129,193},{193,1... | collective-permute-start | bytes 1179656 | tf_op jit(solution)/shard_map/ppermute | solution.py:518
  21.0 2.8 %collective-permute-start.7 = (f32[3,4,64,128]{3,2,1,0:T(8,128)}, f32[3,4,64,128]{3,2,1,0:T(8,128)S(1)}, u32[]{:S(2)}, u32[]{:S(2)}) collective-permute-start(f32[3,4,64,128]{3,2,1,0:T(8,128)} %get-tuple-element.34), channel_id=1, source_target_pairs={{0,192},{64,0},{128,64},{192,128},{1,193},{65,1},{129,65},{193,129... | collective-permute-start | bytes 1179656 | tf_op jit(solution)/shard_map/ppermute | solution.py:517
  23.8 1.0 %collective-permute-done.3.right_in.refs_3_ = f32[5,16,128]{2,1,0:T(8,128)S(1)} collective-permute-done((f32[5,16,128]{2,1,0:T(8,128)S(1)}, f32[5,16,128]{2,1,0:T(8,128)S(1)}, u32[]{:S(2)}, u32[]{:S(2)}) %collective-permute-start.3) | collective-permute-done | bytes 40992 | tf_op jit(solution)/shard_map/ppermute | solution.py:492
  24.8 3.9 %collective-permute-done.2.left_in.refs_2_ = f32[5,16,128]{2,1,0:T(8,128)} collective-permute-done((f32[5,16,128]{2,1,0:T(8,128)S(1)}, f32[5,16,128]{2,1,0:T(8,128)}, u32[]{:S(2)}, u32[]{:S(2)}) %collective-permute-start.2) | collective-permute-done | bytes 40992 | tf_op jit(solution)/shard_map/ppermute | solution.py:491
  28.7 2.8 %shard_map.72 = f32[32,128]{1,0:T(8,128)S(1)} custom-call(s32[1]{0:T(128)} %bitcast.grp.me, s32[16]{0:T(128)S(1)} %copy-done.5, s32[1,64]{1,0:T(1,128)S(1)} %bitcast.11, f32[5,8,64,128]{3,2,1,0:T(8,128)S(1)} %copy-done, f32[3,8,64,128]{3,2,1,0:T(8,128)S(1)} %get-tuple-element.24.curls, f32[5,16,128]{2,1,0:T(8,128)S(1)} %get-tuple-element.26.x_low.refs_0_, ...), custom_call_target="tpu_custom_call" | custom-call | flops 60000002048 | bytes 1000000 | tf_op jit(solution)/shard_map/pallas_call | solution.py:521
  31.5 0.0 copy-start.1
  31.5 0.6 %copy-done.1 = f32[32,128]{1,0:T(8,128)} copy-done((f32[32,128]{1,0:T(8,128)}, f32[32,128]{1,0:T(8,128)S(1)}, u32[]{:S(2)}) %copy-start.1) | copy-done | bytes 16408
  32.1 6.6 %all-to-all-start = ((f32[32,1,128]{2,1,0:T(1,128)}), f32[32,1,128]{2,1,0:T(1,128)S(1)}, u32[]{:S(2)}, u32[]{:S(2)}) async-start(f32[32,1,128]{2,1,0:T(1,128)} %bitcast.9), calls=%async_computation | async-start | bytes 32768 | tf_op jit(solution)/shard_map/all_to_all | solution.py:540
  38.7 1.8 %shard_map.73.partly = f32[5,8,64,128]{3,2,1,0:T(8,128)S(1)} custom-call(f32[5,8,64,128]{3,2,1,0:T(8,128)S(1)} %get-tuple-element.29.partly, f32[5,8,64,128]{3,2,1,0:T(8,128)S(1)} %copy-done, f32[5,16,128]{2,1,0:T(8,128)S(1)} %get-tuple-element.26.x_low.refs_0_, f32[5,16,128]{2,1,0:T(8,128)S(1)} %get-tuple-element.27.x_high.refs_1_, ...), custom_call_target="tpu_custom_call" | custom-call | tf_op jit(solution)/shard_map/pallas_call | solution.py:541
  40.5 0.0 copy-start.2
  40.6 2.2 %shard_map.75 = f32[5,8,64,128]{3,2,1,0:T(8,128)} custom-call(f32[5,8,64,128]{3,2,1,0:T(8,128)S(1)} %shard_map.73.partly, f32[2,4,64,128]{3,2,1,0:T(8,128)} %collective-permute-done.4.below_a.refs_0_, f32[3,4,64,128]{3,2,1,0:T(8,128)S(1)} %collective-permute-done.6.refs_1_, f32[2,4,64,128]{3,2,1,0:T(8,128)} %collective-permute-done.5.above_a.refs_2_, ...), custom_call_target="tpu_custom_call" | custom-call | tf_op jit(solution)/shard_map/pallas_call | solution.py:549
  42.8 3.1 %all-to-all-done = f32[32,1,128]{2,1,0:T(1,128)S(1)} async-done(((f32[32,1,128]{2,1,0:T(1,128)}), f32[32,1,128]{2,1,0:T(1,128)S(1)}, u32[]{:S(2)}, u32[]{:S(2)}) %all-to-all-start) | async-done | bytes 16416 | tf_op jit(solution)/shard_map/all_to_all | solution.py:540
  45.9 1.5 %shard_map.76 = f32[8,4,8]{2,1,0:T(4,128)} custom-call(s32[1]{0:T(128)} %bitcast.grp.me, s32[1]{0:T(128)} %bitcast.2.depth, s32[16]{0:T(128)S(1)} %bitcast.10, s32[1,64]{1,0:T(1,128)S(1)} %bitcast.12, f32[4,8,128]{2,1,0:T(8,128)S(1)} %bitcast.8), custom_call_target="tpu_custom_call" | custom-call | tf_op jit(solution)/shard_map/pallas_call | solution.py:564
  (15 shorter events, 0.1 us)
Async XLA Ops:
  0.6 6.6 %copy-start = (f32[5,8,64,128]{3,2,1,0:T(8,128)S(1)}, f32[5,8,64,128]{3,2,1,0:T(8,128)}, u32[]{:S(2)}) copy-start(f32[5,8,64,128]{3,2,1,0:T(8,128)} %state.8) | copy-start | bytes 3932164
  2.0 18.1 %collective-permute-start.5 = (f32[2,4,64,128]{3,2,1,0:T(8,128)S(1)}, f32[2,4,64,128]{3,2,1,0:T(8,128)}, u32[]{:S(2)}, u32[]{:S(2)}) collective-permute-start(f32[2,4,64,128]{3,2,1,0:T(8,128)S(1)} %get-tuple-element.19), channel_id=1, source_target_pairs={{0,192},{64,0},{128,64},{192,128},{1,193},{65,1},{129,65},{193,129... | collective-permute-start | bytes 786440 | tf_op jit(solution)/shard_map/ppermute | solution.py:481
  7.3 12.9 %collective-permute-start.4 = (f32[2,4,64,128]{3,2,1,0:T(8,128)S(1)}, f32[2,4,64,128]{3,2,1,0:T(8,128)}, u32[]{:S(2)}, u32[]{:S(2)}) collective-permute-start(f32[2,4,64,128]{3,2,1,0:T(8,128)S(1)} %get-tuple-element.28), channel_id=1, source_target_pairs={{0,64},{64,128},{128,192},{192,0},{1,65},{65,129},{129,193},{193,1... | collective-permute-start | bytes 786440 | tf_op jit(solution)/shard_map/ppermute | solution.py:480
  7.3 9.3 %collective-permute-start.1 = (f32[5,4,8,128]{3,2,1,0:T(8,128)S(1)}, f32[5,4,8,128]{3,2,1,0:T(8,128)S(1)}, u32[]{:S(2)}, u32[]{:S(2)}) collective-permute-start(f32[5,4,8,128]{3,2,1,0:T(8,128)S(1)} %get-tuple-element.22), channel_id=1, source_target_pairs={{0,7},{1,0},{2,1},{3,2},{4,3},{5,4},{6,5},{7,6},{8,15},{9,8},{10,9... | collective-permute-start | bytes 245768 | tf_op jit(solution)/shard_map/ppermute | solution.py:483
  8.3 9.4 %collective-permute-start = (f32[5,4,8,128]{3,2,1,0:T(8,128)S(1)}, f32[5,4,8,128]{3,2,1,0:T(8,128)S(1)}, u32[]{:S(2)}, u32[]{:S(2)}) collective-permute-start(f32[5,4,8,128]{3,2,1,0:T(8,128)S(1)} %get-tuple-element.21), channel_id=1, source_target_pairs={{0,1},{1,2},{2,3},{3,4},{4,5},{5,6},{6,7},{7,0},{8,9},{9,10},{10,1... | collective-permute-start | bytes 245768 | tf_op jit(solution)/shard_map/ppermute | solution.py:482
  9.8 15.0 %collective-permute-start.3 = (f32[5,16,128]{2,1,0:T(8,128)S(1)}, f32[5,16,128]{2,1,0:T(8,128)S(1)}, u32[]{:S(2)}, u32[]{:S(2)}) collective-permute-start(f32[5,16,128]{2,1,0:T(8,128)S(1)} %get-tuple-element.26.x_low.refs_0_), channel_id=1, source_target_pairs={{0,56},{8,0},{16,8},{24,16},{32,24},{40,32},{48,40},{56,48},{1,57}... | collective-permute-start | bytes 122888 | tf_op jit(solution)/shard_map/ppermute | solution.py:492
  16.6 12.0 %copy-start.3 = (s32[64]{0:T(128)S(1)}, s32[64]{0:T(128)}, u32[]{:S(2)}) copy-start(s32[64]{0:T(128)} %param.9) | copy-start | bytes 772
  16.6 12.0 %copy-start.4 = (f32[4,4,256]{2,1,0:T(4,128)S(1)}, f32[4,4,256]{2,1,0:T(4,128)}, u32[]{:S(2)}) copy-start(f32[4,4,256]{2,1,0:T(4,128)} %tables.1) | copy-start | bytes 49156
  16.6 12.0 %copy-start.5 = (s32[16]{0:T(128)S(1)}, s32[16]{0:T(128)}, u32[]{:S(2)}) copy-start(s32[16]{0:T(128)} %index.1) | copy-start | bytes 196
  16.7 12.0 %collective-permute-start.2 = (f32[5,16,128]{2,1,0:T(8,128)S(1)}, f32[5,16,128]{2,1,0:T(8,128)}, u32[]{:S(2)}, u32[]{:S(2)}) collective-permute-start(f32[5,16,128]{2,1,0:T(8,128)S(1)} %get-tuple-element.27.x_high.refs_1_), channel_id=1, source_target_pairs={{0,8},{8,16},{16,24},{24,32},{32,40},{40,48},{48,56},{56,0},{1,9},... | collective-permute-start | bytes 122888 | tf_op jit(solution)/shard_map/ppermute | solution.py:491
  20.2 20.4 %collective-permute-start.6 = (f32[3,4,64,128]{3,2,1,0:T(8,128)}, f32[3,4,64,128]{3,2,1,0:T(8,128)S(1)}, u32[]{:S(2)}, u32[]{:S(2)}) collective-permute-start(f32[3,4,64,128]{3,2,1,0:T(8,128)} %get-tuple-element.33), channel_id=1, source_target_pairs={{0,64},{64,128},{128,192},{192,0},{1,65},{65,129},{129,193},{193,1... | collective-permute-start | bytes 1179656 | tf_op jit(solution)/shard_map/ppermute | solution.py:518
  21.0 19.6 %collective-permute-start.7 = (f32[3,4,64,128]{3,2,1,0:T(8,128)}, f32[3,4,64,128]{3,2,1,0:T(8,128)S(1)}, u32[]{:S(2)}, u32[]{:S(2)}) collective-permute-start(f32[3,4,64,128]{3,2,1,0:T(8,128)} %get-tuple-element.34), channel_id=1, source_target_pairs={{0,192},{64,0},{128,64},{192,128},{1,193},{65,1},{129,65},{193,129... | collective-permute-start | bytes 1179656 | tf_op jit(solution)/shard_map/ppermute | solution.py:517
  31.5 0.6 %copy-start.1 = (f32[32,128]{1,0:T(8,128)}, f32[32,128]{1,0:T(8,128)S(1)}, u32[]{:S(2)}) copy-start(f32[32,128]{1,0:T(8,128)S(1)} %shard_map.72) | copy-start | bytes 49156
  32.1 13.8 %all-to-all-start = ((f32[32,1,128]{2,1,0:T(1,128)}), f32[32,1,128]{2,1,0:T(1,128)S(1)}, u32[]{:S(2)}, u32[]{:S(2)}) async-start(f32[32,1,128]{2,1,0:T(1,128)} %bitcast.9), calls=%async_computation | async-start | bytes 32768 | tf_op jit(solution)/shard_map/all_to_all | solution.py:540
  40.5 5.4 %copy-start.2 = (s32[16,1]{0,1:T(1,128)S(1)}, s32[16,1]{0,1:T(1,128)}, u32[]{:S(2)}) copy-start(s32[16,1]{0,1:T(1,128)} %param.7) | copy-start | bytes 196
